TPU v7x, 128 devices: a whole 4x4x4 slice. The times are simulated.
128 devices in a mesh: comp: 2 (over z_hi), gy: 8 (over x, z_lo), gx: 8 (over y, core).
Axes of the slice: x: 4, y: 4, z: 4 (z_hi: 2, z_lo: 2; z = z_hi * 2 + z_lo), core: 2. Of those that a mesh axis runs over, the one named last changes fastest.
Arguments:
- column_water: float32 [2, 16, 64, 1024], P('comp', None, 'gy', 'gx'), may hold values from 0.2 to 2
- land_soil: float32 [2, 64, 1024], P('comp', 'gy', 'gx'), may hold values from 0.1 to 0.9
- level_weight: float32 [16], replicated, may hold values from 0.01 to 0.1
- excess_weight: float32 [16], replicated, may hold values from 0.3 to 3
- soil_weight: float32 [16], replicated, may hold values from 0.3 to 3
- terrain_class: int32 [640, 10240], P('gy', 'gx'), may hold values from 0 to 15
- surface_head: float32 [2, 640, 10240], P('comp', 'gy', 'gx'), may hold values from 0 to 1
- conductivity: float32 [2, 640, 10240], P('comp', 'gy', 'gx'), may hold values from 0.02 to 0.22
- active_mask: int32 [2, 640, 10240], P('comp', 'gy', 'gx'), may hold values 0 or 1
- flow_code: int32 [2, 640, 10240], P('comp', 'gy', 'gx'), may hold values from 0 to 3
Outputs:
- coupled_state: float32 [2, 64, 1024], P('comp', 'gy', 'gx')
All inputs are finite; a program needn't handle non-finite values. No bound on the sum of `active_mask` on one device may be relied on, other than what follows from the above.
Results may differ from a plain program's by a relative error of at most 0.0003.
Values sent between devices are 32-bit elements; how exact they have to be, the bound alone decides.
No kernel may reach another device: no remote copies, remote signals or barrier semaphores. Data moves between devices by JAX's collectives and lax.ppermute only.
A program may use at most 64 MiB of HBM per device.

v0:
```python
import jax
import jax.numpy as jnp
import numpy as np
from jax import lax
from jax.experimental import pallas as pl
from jax.experimental.pallas import tpu as pltpu
from jax.sharding import PartitionSpec as P

AGG = 10
NSUB = 8
LEV = 16
ROWS = 80
COLS = 1280
HALO = 8
STRIPS = 12
TILES = 11
WIDE = TILES * 128
FIELDS = 5
BF = jnp.bfloat16
F32 = jnp.float32

diffusion_rate = 0.2
infiltration_rate = 0.05
drainage_rate = 0.1
half_point = 0.1
evaporation_scale = 0.5


def tables():
    lane = np.arange(WIDE)
    col = np.where(lane < COLS, lane // AGG, np.where(lane < COLS + 8, 128, np.where(lane >= WIDE - 8, 255, -1)))
    up_cols = (np.arange(256)[:, None] == col[None]).astype(np.float32)
    pool_cols = up_cols[:128].T.copy()
    k, s = np.meshgrid(np.arange(STRIPS), np.arange(8), indexing="ij")
    fine = (12 * s + k).reshape(-1)
    row = np.where(fine < ROWS, fine // AGG, np.where(fine < ROWS + 8, 8, 15))
    up_rows = (row[:, None] == np.arange(16)[None]).astype(np.float32)
    pool_rows = up_rows[:, :8].T * (fine < ROWS)[None]
    own_rows = (np.arange(ROWS)[:, None] // AGG == np.arange(8)[None]).astype(np.float32)
    return dict(
        up_cols=jnp.asarray(up_cols, BF),
        pool_cols=jnp.asarray(pool_cols, BF),
        up_rows=jnp.asarray(np.concatenate([up_rows, up_rows], 1), BF),
        pool_rows=jnp.asarray(np.concatenate([pool_rows, pool_rows], 1), BF),
        own_up=jnp.asarray(np.concatenate([own_rows, own_rows], 1), BF),
        own_pool=jnp.asarray(np.concatenate([own_rows.T, own_rows.T], 1), BF),
    )


def split(x):
    high = x.astype(BF)
    return high, (x - high.astype(F32)).astype(BF)


def dot(a, b):
    return jnp.dot(a, b, preferred_element_type=F32)


def lanes():
    return lax.broadcasted_iota(jnp.int32, (8, 128), 1)


def beside(tiles, lane):
    right = [pltpu.roll(x, 1, 1) for x in tiles]
    left = [pltpu.roll(x, 127, 1) for x in tiles]
    n = len(tiles)
    west = [jnp.where(lane == 0, right[t - 1], right[t]) for t in range(n)]
    east = [jnp.where(lane == 127, left[(t + 1) % n], left[t]) for t in range(n)]
    return west, east


def cut(t):
    return slice(t * 128, (t + 1) * 128)


def pack_kernel(
    water, soil, etab, stab, terrain, head, cond, mask, code, pool_cols, up_cols, own_up, own_pool,
    gxl, gxr, main_up, main_down, gyu, gyd, keff_out, ew_out, sw_out, square,
):
    group = lax.axis_index("comp")

    @pl.when(group == 0)
    def _():
        square[...] = water[...].T
        gxl[0:8] = square[0:8]
        gxr[0:8] = square[120:128]
        square[0:8] = soil[...]
        square[8:128] = jnp.zeros((120, 128), F32)
        turned = square[...].T
        gxl[8:16] = turned[0:8]
        gxr[8:16] = turned[120:128]
        gxl[16:40] = jnp.zeros((24, 128), F32)
        gxr[16:40] = jnp.zeros((24, 128), F32)
        for j in range(3):
            for h in range(2):
                at = j * 16 + h * 8
                main_up[at : at + 8] = water[pl.ds(h * 64 + j, 8, stride=8), :]
                main_down[at : at + 8] = water[pl.ds(h * 64 + 5 + j, 8, stride=8), :]
        main_up[48:56] = soil[...]
        main_down[48:56] = soil[...]

    @pl.when(group == 1)
    def _():
        ebig = jnp.broadcast_to(etab[...], (8, 128))
        sbig = jnp.broadcast_to(stab[...], (8, 128))
        for r in range(0, ROWS, 8):
            for t in range(10):
                at = terrain[r : r + 8, cut(t)]
                ew_out[r : r + 8, cut(t)] = jnp.take_along_axis(ebig, at, axis=1)
                sw_out[r : r + 8, cut(t)] = jnp.take_along_axis(sbig, at, axis=1)
        for out in (ew_out, sw_out):
            high, low = split(out[...])
            part = dot(high, pool_cols[0:COLS]) + dot(low, pool_cols[0:COLS])
            high, low = split(part)
            total = dot(own_pool[...], jnp.concatenate([high, low], axis=0))
            high, low = split(float(AGG * AGG) / total)
            wide = dot(jnp.concatenate([high, low], axis=0), up_cols[0:128, 0:COLS]).astype(BF)
            out[...] = out[...] * dot(own_up[...], wide)
        keff_out[...] = cond[...] * mask[...].astype(F32)
        fields = (
            lambda r, c: keff_out[r, c],
            lambda r, c: head[r, c],
            lambda r, c: code[r, c].astype(F32),
            lambda r, c: ew_out[r, c],
            lambda r, c: sw_out[r, c],
        )
        for f, field in enumerate(fields):
            for t in range(10):
                at = f * 80 + t * 8
                gyu[at : at + 8] = field(slice(0, 8), cut(t))
                gyd[at : at + 8] = field(slice(ROWS - 8, ROWS), cut(t))
        lane = lax.broadcasted_iota(jnp.int32, (ROWS, 128), 1)
        edges = jnp.zeros((ROWS, 128), F32)
        for f, field in enumerate(fields):
            first = field(slice(0, ROWS), cut(0))
            last = field(slice(0, ROWS), cut(9))
            first = first if f == 0 else pltpu.roll(first, 8 * f, 1)
            last = pltpu.roll(last, (64 + 8 * f - 120) % 128, 1)
            edges = jnp.where(lane // 8 == f, first, edges)
            edges = jnp.where(lane // 8 == 8 + f, last, edges)
        square[0:ROWS] = edges
        square[ROWS:128] = jnp.zeros((128 - ROWS, 128), F32)
        square[...] = square[...].T
        gxl[...] = square[0:40]
        gxr[...] = square[64:104]


def middle_kernel(
    water, soil, weight, keff, head, code, ew, sw, from_left, from_right, from_up, from_down, rows_up, rows_down,
    coarse, water_out, a_e, a_w, a_n, a_s, a_c, m_e, m_w, m_n, m_s, m_c, head_out, ew_out, sw_out,
    square, side, nat, kring, cring,
):
    group = lax.axis_index("comp")
    gy, gx = lax.axis_index("gy"), lax.axis_index("gx")
    has_up = (gy > 0).astype(F32)
    has_down = (gy < lax.axis_size("gy") - 1).astype(F32)
    has_left = (gx > 0).astype(F32)
    has_right = (gx < lax.axis_size("gx") - 1).astype(F32)

    @pl.when(group == 0)
    def _():
        pairs = (
            (from_right[0:8], from_left[0:8]),
            (from_down[16:24], from_down[0:8]),
            (from_up[16:24], from_up[0:8]),
        )
        square[8:120] = jnp.zeros((112, 128), F32)
        for i, (right, left) in enumerate(pairs):
            square[0:8] = right
            square[120:128] = left
            side[i] = square[...].T
        lane = lanes()
        for at, (own, down, up) in (
            (0, (from_right[8:16], from_down[24:32], from_up[24:32])),
            (120, (from_left[8:16], from_down[8:16], from_up[8:16])),
        ):
            square[at : at + 8] = jnp.where(
                lane < 8, own, jnp.where(lane < 16, pltpu.roll(down, 8, 1), pltpu.roll(up, 16, 1))
            )
        side_soil = square[...].T

        lane2 = lax.broadcasted_iota(jnp.int32, (1, 256), 1)
        col_ok = jnp.where(lane2 < 128, 1.0, jnp.where(lane2 < 192, has_right, has_left))

        def levels(ref, row):
            return jnp.concatenate(
                [ref[pl.ds(h * 64 + row, 8, stride=8), :] for h in range(2)], axis=0
            )

        def side_levels(i, row):
            return jnp.concatenate(
                [side[i, pl.ds(h * 64 + row, 8, stride=8), :] for h in range(2)], axis=0
            )

        field = []
        for j in range(3):
            tile = from_up[32 + j * 16 : 48 + j * 16]
            field.append(jnp.concatenate([tile, side_levels(2, 5 + j)], axis=1) * (col_ok * has_up))
        for j in range(8):
            field.append(jnp.concatenate([levels(water, j), side_levels(0, j)], axis=1) * col_ok)
        for j in range(3):
            tile = from_down[32 + j * 16 : 48 + j * 16]
            field.append(jnp.concatenate([tile, side_levels(1, j)], axis=1) * (col_ok * has_down))

        def sweep(old, first, last):
            new = {}
            for q in range(first, last):
                around = old[q - 1] + old[q + 1] + pltpu.roll(old[q], 1, 1) + pltpu.roll(old[q], 255, 1)
                new[q] = old[q] + diffusion_rate * (around - 4.0 * old[q])
            return new

        once = sweep(field, 1, 13)
        for q in once:
            once[q] = once[q] * (col_ok * (has_up if q < 3 else has_down if q > 10 else 1.0))
        twice = sweep(once, 2, 12)
        for j in range(8):
            water_out[j : j + 1] = twice[3 + j][0:1, 0:128]
        level_weight = jnp.broadcast_to(weight[...], (LEV, 256))
        rain = {q: jnp.sum(level_weight * twice[q] * twice[q], axis=0, keepdims=True) for q in twice}
        blank = jnp.zeros((6, 256), F32)
        rain = jnp.concatenate([rain[3 + j] for j in range(8)] + [rain[11], blank, rain[2]], axis=0)
        moist = jnp.concatenate(
            [
                jnp.concatenate([soil[...], side_soil[0:8]], axis=1),
                jnp.concatenate([from_down[80:81], side_soil[8:9]], axis=1),
                blank,
                jnp.concatenate([from_up[87:88], side_soil[23:24]], axis=1),
            ],
            axis=0,
        )
        coarse[0] = rain * moist * moist / (moist * moist + half_point)
        coarse[1] = moist

    @pl.when(group == 1)
    def _():
        lane128 = lax.broadcasted_iota(jnp.int32, (40, 128), 1)

        def column(own, down, up):
            down, up = pltpu.roll(down, 80, 1), pltpu.roll(up, 16, 1)
            return jnp.where(lane128 < 80, own, jnp.where(lane128 < 88, down * has_down, up * has_up))

        square[...] = jnp.zeros((128, 128), F32)
        square[0:40] = column(from_right[...], from_down[40:80], from_up[40:80]) * has_right
        square[64:104] = column(from_left[...], from_down[0:40], from_up[0:40]) * has_left
        side[0] = square[...].T
        own = (
            lambda c: keff[:, c],
            lambda c: head[:, c],
            lambda c: code[:, c].astype(F32),
            lambda c: ew[:, c],
            lambda c: sw[:, c],
        )
        lane = lax.broadcasted_iota(jnp.int32, (96, 128), 1)
        for f in range(FIELDS):
            for t in range(10):
                at = f * 80 + t * 8
                nat[t, 0:ROWS] = own[f](cut(t))
                nat[t, ROWS : ROWS + 8] = rows_down[at : at + 8] * has_down
                nat[t, ROWS + 8 : ROWS + 16] = rows_up[at : at + 8] * has_up
            columns = side[0, 0:96]
            right = columns if f == 0 else pltpu.roll(columns, (-8 * f) % 128, 1)
            left = pltpu.roll(columns, 120 - 64 - 8 * f, 1)
            nat[10] = jnp.where(lane < 8, right, jnp.where(lane >= 120, left, 0.0))
            for k in range(STRIPS):
                for t in range(TILES):
                    value = nat[t, pl.ds(k, 8, stride=STRIPS), :]
                    if f == 0:
                        kring[k + 1, :, cut(t)] = value
                    elif f == 1:
                        active = kring[k + 1, :, cut(t)] > 0.0
                        head_out[k, :, cut(t)] = jnp.where(active, value, 0.0)
                    elif f == 2:
                        cring[k + 1, :, cut(t)] = value
                    elif f == 3:
                        active = kring[k + 1, :, cut(t)] > 0.0
                        ew_out[k, :, cut(t)] = jnp.where(active, value, 0.0)
                    else:
                        sw_out[k, :, cut(t)] = value
        for ring in (kring, cring):
            for t in range(TILES):
                ring[0, :, cut(t)] = pltpu.roll(ring[STRIPS, :, cut(t)], 1, 0)
                ring[STRIPS + 1, :, cut(t)] = pltpu.roll(ring[1, :, cut(t)], 7, 0)

        def strip(k, carry):
            lane = lanes()
            here = [kring[k + 1, :, cut(t)] for t in range(TILES)]
            codes = [cring[k + 1, :, cut(t)] for t in range(TILES)]
            west, east = beside(here, lane)

            def drains(cond, codes, number):
                return jnp.where((cond > 0.0) & (codes == number), drainage_rate, 0.0)

            to_east, _ = beside([drains(here[t], codes[t], 3.0) for t in range(TILES)], lane)
            _, to_west = beside([drains(here[t], codes[t], 2.0) for t in range(TILES)], lane)
            for t in range(TILES):
                north, south = kring[k, :, cut(t)], kring[k + 2, :, cut(t)]
                n, s = jnp.sqrt(here[t] * north), jnp.sqrt(here[t] * south)
                w, e = jnp.sqrt(here[t] * west[t]), jnp.sqrt(here[t] * east[t])
                a_n[k, :, cut(t)] = n
                a_s[k, :, cut(t)] = s
                a_w[k, :, cut(t)] = w
                a_e[k, :, cut(t)] = e
                a_c[k, :, cut(t)] = 1.0 - ((n + s) + (w + e))
                m_n[k, :, cut(t)] = drains(north, cring[k, :, cut(t)], 1.0)
                m_s[k, :, cut(t)] = drains(south, cring[k + 2, :, cut(t)], 0.0)
                m_w[k, :, cut(t)] = to_east[t]
                m_e[k, :, cut(t)] = to_west[t]
                m_c[k, :, cut(t)] = jnp.where(here[t] > 0.0, drainage_rate, 0.0)
            return carry

        lax.fori_loop(0, STRIPS, strip, 0)


def route_kernel(
    coarse, a_e, a_w, a_n, a_s, a_c, m_e, m_w, m_n, m_s, m_c, head, ew, sw, up_cols, up_rows, pool_cols, pool_rows,
    ponded_out, stored_out, pond_a, pond_b, store_a, store_b,
):
    group = lax.axis_index("comp")

    @pl.when(group == 1)
    def _():
        pieces = jnp.concatenate([*split(coarse[0]), *split(coarse[1])], axis=0)
        wide = dot(pieces, up_cols[...]).astype(BF)
        excess = dot(up_rows[...], wide[0:32])
        moist = dot(up_rows[...], wide[32:64])
        pond_a[1 : STRIPS + 1] = head[...] + ew[...] * excess.reshape(STRIPS, 8, WIDE)
        store_a[1 : STRIPS + 1] = sw[...] * moist.reshape(STRIPS, 8, WIDE)

        def close(ring):
            for t in range(TILES):
                ring[0, :, cut(t)] = pltpu.roll(ring[STRIPS, :, cut(t)], 1, 0)
                ring[STRIPS + 1, :, cut(t)] = pltpu.roll(ring[1, :, cut(t)], 7, 0)

        close(pond_a)
        close(store_a)

        def substep(pond, store, new_pond, new_store):
            def strip(k, carry):
                lane = lanes()
                p = [pond[k + 1, :, cut(t)] for t in range(TILES)]
                s = [store[k + 1, :, cut(t)] for t in range(TILES)]
                q = [x * x for x in s]
                p_w, p_e = beside(p, lane)
                q_w, q_e = beside(q, lane)
                for t in range(TILES):
                    c = cut(t)
                    s_n, s_s = store[k, :, c], store[k + 2, :, c]
                    below = 1.0 + s[t]
                    guess = pl.reciprocal(below, approx=True)
                    guess = guess * (2.0 - below * guess)
                    soaked = infiltration_rate * p[t] * guess
                    flow = a_n[k, :, c] * pond[k, :, c] + a_s[k, :, c] * pond[k + 2, :, c]
                    flow = flow + (a_w[k, :, c] * p_w[t] + a_e[k, :, c] * p_e[t])
                    new_pond[k + 1, :, c] = a_c[k, :, c] * p[t] + flow - soaked
                    inflow = m_n[k, :, c] * (s_n * s_n) + m_s[k, :, c] * (s_s * s_s)
                    inflow = inflow + (m_w[k, :, c] * q_w[t] + m_e[k, :, c] * q_e[t])
                    new_store[k + 1, :, c] = s[t] + soaked - m_c[k, :, c] * q[t] + inflow
                return carry

            lax.fori_loop(0, STRIPS, strip, 0)
            close(new_pond)
            close(new_store)

        def two(i, carry):
            substep(pond_a, store_a, pond_b, store_b)
            substep(pond_b, store_b, pond_a, store_a)
            return carry

        lax.fori_loop(0, NSUB // 2, two, 0)
        for ring, out in ((pond_a, ponded_out), (store_a, stored_out)):
            high, low = split(ring[1 : STRIPS + 1].reshape(STRIPS * 8, WIDE))
            part = dot(high, pool_cols[...]) + dot(low, pool_cols[...])
            out[...] = dot(pool_rows[...], jnp.concatenate([*split(part)], axis=0)) * (1.0 / (AGG * AGG))


def moved(array, mesh_shape, target):
    groups, ys, xs = mesh_shape
    pairs = []
    for g in range(groups):
        for y in range(ys):
            for x in range(xs):
                a, b, c = target(g, y, x)
                pairs.append(((g * ys + y) * xs + x, ((a % groups) * ys + b % ys) * xs + c % xs))
    return lax.ppermute(array, ("comp", "gy", "gx"), pairs)


def f32(*shape):
    return jax.ShapeDtypeStruct(shape, F32)


def per_device(
    column_water,
    land_soil,
    level_weight,
    excess_weight,
    soil_weight,
    terrain_class,
    surface_head,
    conductivity,
    active_mask,
    flow_code,
):
    shape = tuple(lax.axis_size(axis) for axis in ("comp", "gy", "gx"))
    group = lax.axis_index("comp")
    m = tables()
    water = column_water[0].reshape(128, 128)
    soil = land_soil[0]
    etab = jnp.pad(excess_weight, (0, 112))[None]
    stab = jnp.pad(soil_weight, (0, 112))[None]
    params = pltpu.CompilerParams(vmem_limit_bytes=32 * 1024 * 1024)
    gxl, gxr, main_up, main_down, gyu, gyd, keff, ew, sw = pl.pallas_call(
        pack_kernel,
        out_shape=[f32(40, 128)] * 2 + [f32(56, 128)] * 2 + [f32(400, 128)] * 2 + [f32(ROWS, COLS)] * 3,
        scratch_shapes=[pltpu.VMEM((128, 128), F32)],
        compiler_params=params,
        name="pack",
    )(
        water, soil, etab, stab, terrain_class, surface_head[0], conductivity[0], active_mask[0], flow_code[0],
        m["pool_cols"], m["up_cols"], m["own_up"], m["own_pool"],
    )
    from_left = moved(gxr, shape, lambda g, y, x: (g, y, x + 1))
    from_right = moved(gxl, shape, lambda g, y, x: (g, y, x - 1))
    rows_up = moved(gyd, shape, lambda g, y, x: (g, y + g, x))
    rows_down = moved(gyu, shape, lambda g, y, x: (g, y - g, x))
    land = jnp.concatenate([from_left[:16], from_right[:16]])
    route = jnp.concatenate([from_left, from_right, jnp.zeros((8, 128), F32)])
    send_up = jnp.where(group == 0, jnp.concatenate([land, main_up]), route)
    send_down = jnp.where(group == 0, jnp.concatenate([land, main_down]), route)
    from_up = moved(send_down, shape, lambda g, y, x: (g, y + 1, x))
    from_down = moved(send_up, shape, lambda g, y, x: (g, y - 1, x))
    strips = f32(STRIPS, 8, WIDE)
    coarse, water_top, *prepared = pl.pallas_call(
        middle_kernel,
        out_shape=[f32(2, 16, 256), f32(8, 128)] + [strips] * 13,
        scratch_shapes=[
            pltpu.VMEM((128, 128), F32),
            pltpu.VMEM((3, 128, 128), F32),
            pltpu.VMEM((TILES, 96, 128), F32),
            pltpu.VMEM((STRIPS + 2, 8, WIDE), F32),
            pltpu.VMEM((STRIPS + 2, 8, WIDE), F32),
        ],
        compiler_params=params,
        name="middle",
    )(
        water, soil, level_weight[:, None], keff, surface_head[0], flow_code[0], ew, sw,
        from_left, from_right, from_up, from_down, rows_up, rows_down,
    )
    arrived = moved(coarse, shape, lambda g, y, x: (1 - g, y, x))
    ring = pltpu.VMEM((STRIPS + 2, 8, WIDE), F32)
    ponded, stored = pl.pallas_call(
        route_kernel,
        out_shape=[f32(8, 128), f32(8, 128)],
        scratch_shapes=[ring] * 4,
        compiler_params=params,
        name="route",
    )(arrived, *prepared, m["up_cols"], m["up_rows"], m["pool_cols"], m["pool_rows"])
    returned = moved(stored, shape, lambda g, y, x: (1 - g, y, x))
    land_out = returned / (1.0 + evaporation_scale * water_top * water_top)
    return jnp.where(group == 0, land_out, ponded)[None]


def solution(mesh):
    in_specs = (
        P("comp", None, "gy", "gx"),
        P("comp", "gy", "gx"),
        P(),
        P(),
        P(),
        P("gy", "gx"),
        P("comp", "gy", "gx"),
        P("comp", "gy", "gx"),
        P("comp", "gy", "gx"),
        P("comp", "gy", "gx"),
    )
    out_specs = P("comp", "gy", "gx")
    return jax.shard_map(
        per_device, mesh=mesh, in_specs=in_specs, out_specs=out_specs, check_vma=False
    )
```

profile of v0, /device:TPU:0, one launch (start us, length us, event | category | flops | bytes accessed | tf_op | source)
XLA Modules:
  0.0 57.0 jit_solution(2279407280765244840)
XLA Ops:
  0.0 0.7 %pad_bitcast_fusion = (f32[1,128]{1,0:T(1,128)S(1)}, f32[1,128]{1,0:T(1,128)S(1)}) fusion(f32[16]{0:T(128)} %param.20, f32[16]{0:T(128)} %param.19), kind=kLoop, calls=%fused_computation.10 | loop fusion | bytes 1152 | tf_op jit(solution)/shard_map/broadcast_in_dim | solution.py:409
  0.7 0.0 copy-done.14
  0.7 0.7 %copy-done.17 = bf16[8,160]{1,0:T(8,128)(2,1)S(1)} copy-done((bf16[8,160]{1,0:T(8,128)(2,1)S(1)}, bf16[8,160]{1,0:T(8,128)(2,1)}, u32[]{:S(2)}) %copy-start.17) | copy-done | bytes 2584
  1.4 0.0 copy-done.15
  1.4 1.1 %copy-done = bf16[256,1408]{1,0:T(8,128)(2,1)S(1)} copy-done((bf16[256,1408]{1,0:T(8,128)(2,1)S(1)}, bf16[256,1408]{1,0:T(8,128)(2,1)}, u32[]{:S(2)}) %copy-start) | copy-done | bytes 720920
  2.5 1.0 %copy-done.2 = f32[1,80,1280]{2,1,0:T(8,128)S(1)} copy-done((f32[1,80,1280]{2,1,0:T(8,128)S(1)}, f32[1,80,1280]{2,1,0:T(8,128)}, u32[]{:S(2)}) %copy-start.2) | copy-done | bytes 409624
  3.5 1.0 %copy-done.4 = s32[1,80,1280]{2,1,0:T(8,128)S(1)} copy-done((s32[1,80,1280]{2,1,0:T(8,128)S(1)}, s32[1,80,1280]{2,1,0:T(8,128)}, u32[]{:S(2)}) %copy-start.4) | copy-done | bytes 409624
  4.5 1.0 %copy-done.6 = bf16[1408,128]{1,0:T(8,128)(2,1)S(1)} copy-done((bf16[1408,128]{1,0:T(8,128)(2,1)S(1)}, bf16[1408,128]{1,0:T(8,128)(2,1)}, u32[]{:S(2)}) %copy-start.6) | copy-done | bytes 360472
  5.5 1.0 %copy-done.8 = s32[80,1280]{1,0:T(8,128)S(1)} copy-done((s32[80,1280]{1,0:T(8,128)S(1)}, s32[80,1280]{1,0:T(8,128)}, u32[]{:S(2)}) %copy-start.8) | copy-done | bytes 409624
  6.5 1.0 %copy-done.9 = f32[1,80,1280]{2,1,0:T(8,128)S(1)} copy-done((f32[1,80,1280]{2,1,0:T(8,128)S(1)}, f32[1,80,1280]{2,1,0:T(8,128)}, u32[]{:S(2)}) %copy-start.9) | copy-done | bytes 409624
  7.5 1.0 %copy-done.10 = s32[1,80,1280]{2,1,0:T(8,128)S(1)} copy-done((s32[1,80,1280]{2,1,0:T(8,128)S(1)}, s32[1,80,1280]{2,1,0:T(8,128)}, u32[]{:S(2)}) %copy-start.10) | copy-done | bytes 409624
  8.5 0.8 %copy-done.11 = f32[1,16,8,128]{3,2,1,0:T(8,128)S(1)} copy-done((f32[1,16,8,128]{3,2,1,0:T(8,128)S(1)}, f32[1,16,8,128]{3,2,1,0:T(8,128)}, u32[]{:S(2)}) %copy-start.11) | copy-done | bytes 65560
  9.3 0.1 pack.1
  9.4 0.0 collective-permute-start
  9.5 2.9 %collective-permute-start.1 = (f32[40,128]{1,0:T(8,128)S(1)}, f32[40,128]{1,0:T(8,128)S(1)}, u32[]{:S(2)}, u32[]{:S(2)}) collective-permute-start(f32[40,128]{1,0:T(8,128)S(1)} %get-tuple-element.35), channel_id=1, source_target_pairs={{0,7},{1,0},{2,1},{3,2},{4,3},{5,4},{6,5},{7,6},{8,15},{9,8},{10,9... | collective-permute-start | bytes 61448 | tf_op jit(solution)/shard_map/ppermute | solution.py:384
  12.4 0.7 %collective-permute-start.4 = (f32[400,128]{1,0:T(8,128)S(1)}, f32[400,128]{1,0:T(8,128)S(1)}, u32[]{:S(2)}, u32[]{:S(2)}) collective-permute-start(f32[400,128]{1,0:T(8,128)S(1)} %get-tuple-element.38), channel_id=1, source_target_pairs={{0,0},{1,1},{2,2},{3,3},{4,4},{5,5},{6,6},{7,7},{8,8},{9,9},{10,10... | collective-permute-start | bytes 614408 | tf_op jit(solution)/shard_map/ppermute | solution.py:384
  13.1 0.7 %collective-permute-start.5 = (f32[400,128]{1,0:T(8,128)S(1)}, f32[400,128]{1,0:T(8,128)S(1)}, u32[]{:S(2)}, u32[]{:S(2)}) collective-permute-start(f32[400,128]{1,0:T(8,128)S(1)} %get-tuple-element.39), channel_id=1, source_target_pairs={{0,0},{1,1},{2,2},{3,3},{4,4},{5,5},{6,6},{7,7},{8,8},{9,9},{10,10... | collective-permute-start | bytes 614408 | tf_op jit(solution)/shard_map/ppermute | solution.py:384
  13.8 0.1 pad.14.clone
  13.9 0.0 collective-permute-done.from_left
  13.9 0.0 collective-permute-done.1.from_right
  13.9 0.1 fusion.1
  14.0 4.3 %collective-permute-start.3 = (f32[88,128]{1,0:T(8,128)S(1)}, f32[88,128]{1,0:T(8,128)S(1)}, u32[]{:S(2)}, u32[]{:S(2)}) collective-permute-start(f32[88,128]{1,0:T(8,128)S(1)} %get-tuple-element.57), channel_id=1, source_target_pairs={{0,56},{1,57},{2,58},{3,59},{4,60},{5,61},{6,62},{7,63},{8,0},{9,1... | collective-permute-start | bytes 135176 | tf_op jit(solution)/shard_map/ppermute | solution.py:384
  18.2 0.7 %copy-done.18 = f32[16]{0:T(128)S(1)} copy-done((f32[16]{0:T(128)S(1)}, f32[16]{0:T(128)}, u32[]{:S(2)}) %copy-start.18) | copy-done | bytes 88
  18.9 0.1 copy.17.weight
  19.0 1.0 %collective-permute-done.3.from_down = f32[88,128]{1,0:T(8,128)S(1)} collective-permute-done((f32[88,128]{1,0:T(8,128)S(1)}, f32[88,128]{1,0:T(8,128)S(1)}, u32[]{:S(2)}, u32[]{:S(2)}) %collective-permute-start.3) | collective-permute-done | bytes 45088 | tf_op jit(solution)/shard_map/ppermute | solution.py:384
  20.0 4.4 %collective-permute-done.2.from_up = f32[88,128]{1,0:T(8,128)S(1)} collective-permute-done((f32[88,128]{1,0:T(8,128)S(1)}, f32[88,128]{1,0:T(8,128)S(1)}, u32[]{:S(2)}, u32[]{:S(2)}) %collective-permute-start.2) | collective-permute-done | bytes 45088 | tf_op jit(solution)/shard_map/ppermute | solution.py:384
  24.5 0.5 middle.1
  25.0 11.4 %collective-permute-start.6 = (f32[2,16,256]{2,1,0:T(8,128)S(1)}, f32[2,16,256]{2,1,0:T(8,128)S(1)}, u32[]{:S(2)}, u32[]{:S(2)}) collective-permute-start(f32[2,16,256]{2,1,0:T(8,128)S(1)} %get-tuple-element.40), channel_id=1, source_target_pairs={{0,64},{1,65},{2,66},{3,67},{4,68},{5,69},{6,70},{7,71},{8,72},{9,... | collective-permute-start | bytes 98312 | tf_op jit(solution)/shard_map/ppermute | solution.py:384
  36.4 1.9 %collective-permute-done.6.coarse = f32[2,16,256]{2,1,0:T(8,128)S(1)} collective-permute-done((f32[2,16,256]{2,1,0:T(8,128)S(1)}, f32[2,16,256]{2,1,0:T(8,128)S(1)}, u32[]{:S(2)}, u32[]{:S(2)}) %collective-permute-start.6) | collective-permute-done | bytes 32800 | tf_op jit(solution)/shard_map/ppermute | solution.py:384
  38.3 16.5 %collective-permute-start.7 = (f32[8,128]{1,0:T(8,128)S(1)}, f32[8,128]{1,0:T(8,128)S(1)}, u32[]{:S(2)}, u32[]{:S(2)}) collective-permute-start(f32[8,128]{1,0:T(8,128)S(1)} %get-tuple-element.54), channel_id=1, source_target_pairs={{0,64},{1,65},{2,66},{3,67},{4,68},{5,69},{6,70},{7,71},{8,72},{9,... | collective-permute-start | bytes 12296 | tf_op jit(solution)/shard_map/ppermute | solution.py:384
  54.8 1.6 %collective-permute-done.7 = f32[8,128]{1,0:T(8,128)S(1)} collective-permute-done((f32[8,128]{1,0:T(8,128)S(1)}, f32[8,128]{1,0:T(8,128)S(1)}, u32[]{:S(2)}, u32[]{:S(2)}) %collective-permute-start.7) | collective-permute-done | bytes 4128 | tf_op jit(solution)/shard_map/ppermute | solution.py:384
  56.4 0.6 %fusion.5 = f32[1,8,128]{2,1,0:T(8,128)} fusion(f32[8,128]{1,0:T(8,128)S(1)} %get-tuple-element.56, f32[8,128]{1,0:T(8,128)S(1)} %collective-permute-done.7, f32[8,128]{1,0:T(8,128)S(1)} %get-tuple-element.55, pred[]{:T(512)S(6)} %eq.2), kind=kLoop, calls=%fused_computation.9 | loop fusion | flops 5120 | bytes 16385 | tf_op jit(solution)/shard_map/broadcast_in_dim | solution.py:459
  (33 shorter events, 0.1 us)
Async XLA Ops:
  0.0 0.7 %copy-start.14 = (bf16[80,16]{1,0:T(8,128)(2,1)S(1)}, bf16[80,16]{1,0:T(8,128)(2,1)}, u32[]{:S(2)}) copy-start(bf16[80,16]{1,0:T(8,128)(2,1)} %constant.31.clone.own_up) | copy-start | bytes 7684
  0.7 0.7 %copy-start.17 = (bf16[8,160]{1,0:T(8,128)(2,1)S(1)}, bf16[8,160]{1,0:T(8,128)(2,1)}, u32[]{:S(2)}) copy-start(bf16[8,160]{1,0:T(8,128)(2,1)} %constant.32.clone.own_pool) | copy-start | bytes 7684
  0.7 0.7 %copy-start.15 = (f32[1,8,128]{2,1,0:T(8,128)S(1)}, f32[1,8,128]{2,1,0:T(8,128)}, u32[]{:S(2)}) copy-start(f32[1,8,128]{2,1,0:T(8,128)} %param.17) | copy-start | bytes 12292
  1.4 1.1 %copy-start = (bf16[256,1408]{1,0:T(8,128)(2,1)S(1)}, bf16[256,1408]{1,0:T(8,128)(2,1)}, u32[]{:S(2)}) copy-start(bf16[256,1408]{1,0:T(8,128)(2,1)} %constant.27.clone.up_cols) | copy-start | bytes 2162692
  2.5 1.0 %copy-start.2 = (f32[1,80,1280]{2,1,0:T(8,128)S(1)}, f32[1,80,1280]{2,1,0:T(8,128)}, u32[]{:S(2)}) copy-start(f32[1,80,1280]{2,1,0:T(8,128)} %param.22) | copy-start | bytes 1228804
  3.5 1.0 %copy-start.4 = (s32[1,80,1280]{2,1,0:T(8,128)S(1)}, s32[1,80,1280]{2,1,0:T(8,128)}, u32[]{:S(2)}) copy-start(s32[1,80,1280]{2,1,0:T(8,128)} %param.25) | copy-start | bytes 1228804
  4.5 1.0 %copy-start.6 = (bf16[1408,128]{1,0:T(8,128)(2,1)S(1)}, bf16[1408,128]{1,0:T(8,128)(2,1)}, u32[]{:S(2)}) copy-start(bf16[1408,128]{1,0:T(8,128)(2,1)} %constant.28.clone.pool_cols) | copy-start | bytes 1081348
  5.5 1.0 %copy-start.8 = (s32[80,1280]{1,0:T(8,128)S(1)}, s32[80,1280]{1,0:T(8,128)}, u32[]{:S(2)}) copy-start(s32[80,1280]{1,0:T(8,128)} %terrain.1) | copy-start | bytes 1228804
  6.5 1.0 %copy-start.9 = (f32[1,80,1280]{2,1,0:T(8,128)S(1)}, f32[1,80,1280]{2,1,0:T(8,128)}, u32[]{:S(2)}) copy-start(f32[1,80,1280]{2,1,0:T(8,128)} %param.23) | copy-start | bytes 1228804
  7.5 1.0 %copy-start.10 = (s32[1,80,1280]{2,1,0:T(8,128)S(1)}, s32[1,80,1280]{2,1,0:T(8,128)}, u32[]{:S(2)}) copy-start(s32[1,80,1280]{2,1,0:T(8,128)} %param.24) | copy-start | bytes 1228804
  8.5 0.8 %copy-start.11 = (f32[1,16,8,128]{3,2,1,0:T(8,128)S(1)}, f32[1,16,8,128]{3,2,1,0:T(8,128)}, u32[]{:S(2)}) copy-start(f32[1,16,8,128]{3,2,1,0:T(8,128)} %param.16) | copy-start | bytes 196612
  9.3 15.1 %copy-start.3 = (f32[1,80,1280]{2,1,0:T(8,128)S(1)}, f32[1,80,1280]{2,1,0:T(8,128)}, u32[]{:S(2)}) copy-start(f32[1,80,1280]{2,1,0:T(8,128)} %param.22) | copy-start | bytes 1228804
  9.3 15.1 %copy-start.5 = (s32[1,80,1280]{2,1,0:T(8,128)S(1)}, s32[1,80,1280]{2,1,0:T(8,128)}, u32[]{:S(2)}) copy-start(s32[1,80,1280]{2,1,0:T(8,128)} %param.25) | copy-start | bytes 1228804
  9.4 4.4 %collective-permute-start = (f32[40,128]{1,0:T(8,128)S(1)}, f32[40,128]{1,0:T(8,128)S(1)}, u32[]{:S(2)}, u32[]{:S(2)}) collective-permute-start(f32[40,128]{1,0:T(8,128)S(1)} %get-tuple-element.34), channel_id=1, source_target_pairs={{0,1},{1,2},{2,3},{3,4},{4,5},{5,6},{6,7},{7,0},{8,9},{9,10},{10,1... | collective-permute-start | bytes 61448 | tf_op jit(solution)/shard_map/ppermute | solution.py:384
  9.5 4.4 %collective-permute-start.1 = (f32[40,128]{1,0:T(8,128)S(1)}, f32[40,128]{1,0:T(8,128)S(1)}, u32[]{:S(2)}, u32[]{:S(2)}) collective-permute-start(f32[40,128]{1,0:T(8,128)S(1)} %get-tuple-element.35), channel_id=1, source_target_pairs={{0,7},{1,0},{2,1},{3,2},{4,3},{5,4},{6,5},{7,6},{8,15},{9,8},{10,9... | collective-permute-start | bytes 61448 | tf_op jit(solution)/shard_map/ppermute | solution.py:384
  12.4 12.0 %collective-permute-start.4 = (f32[400,128]{1,0:T(8,128)S(1)}, f32[400,128]{1,0:T(8,128)S(1)}, u32[]{:S(2)}, u32[]{:S(2)}) collective-permute-start(f32[400,128]{1,0:T(8,128)S(1)} %get-tuple-element.38), channel_id=1, source_target_pairs={{0,0},{1,1},{2,2},{3,3},{4,4},{5,5},{6,6},{7,7},{8,8},{9,9},{10,10... | collective-permute-start | bytes 614408 | tf_op jit(solution)/shard_map/ppermute | solution.py:384
  13.1 11.3 %collective-permute-start.5 = (f32[400,128]{1,0:T(8,128)S(1)}, f32[400,128]{1,0:T(8,128)S(1)}, u32[]{:S(2)}, u32[]{:S(2)}) collective-permute-start(f32[400,128]{1,0:T(8,128)S(1)} %get-tuple-element.39), channel_id=1, source_target_pairs={{0,0},{1,1},{2,2},{3,3},{4,4},{5,5},{6,6},{7,7},{8,8},{9,9},{10,10... | collective-permute-start | bytes 614408 | tf_op jit(solution)/shard_map/ppermute | solution.py:384
  13.9 10.5 %copy-start.12 = (f32[1,16,8,128]{3,2,1,0:T(8,128)S(1)}, f32[1,16,8,128]{3,2,1,0:T(8,128)}, u32[]{:S(2)}) copy-start(f32[1,16,8,128]{3,2,1,0:T(8,128)} %param.16) | copy-start | bytes 196612
  14.0 6.0 %collective-permute-start.3 = (f32[88,128]{1,0:T(8,128)S(1)}, f32[88,128]{1,0:T(8,128)S(1)}, u32[]{:S(2)}, u32[]{:S(2)}) collective-permute-start(f32[88,128]{1,0:T(8,128)S(1)} %get-tuple-element.57), channel_id=1, source_target_pairs={{0,56},{1,57},{2,58},{3,59},{4,60},{5,61},{6,62},{7,63},{8,0},{9,1... | collective-permute-start | bytes 135176 | tf_op jit(solution)/shard_map/ppermute | solution.py:384
  18.2 0.7 %copy-start.18 = (f32[16]{0:T(128)S(1)}, f32[16]{0:T(128)}, u32[]{:S(2)}) copy-start(f32[16]{0:T(128)} %param.18) | copy-start | bytes 196
  18.2 6.2 %collective-permute-start.2 = (f32[88,128]{1,0:T(8,128)S(1)}, f32[88,128]{1,0:T(8,128)S(1)}, u32[]{:S(2)}, u32[]{:S(2)}) collective-permute-start(f32[88,128]{1,0:T(8,128)S(1)} %get-tuple-element.58), channel_id=1, source_target_pairs={{0,8},{1,9},{2,10},{3,11},{4,12},{5,13},{6,14},{7,15},{8,16},{9,17... | collective-permute-start | bytes 135176 | tf_op jit(solution)/shard_map/ppermute | solution.py:384
  24.4 13.8 %copy-start.1 = (bf16[256,1408]{1,0:T(8,128)(2,1)S(1)}, bf16[256,1408]{1,0:T(8,128)(2,1)}, u32[]{:S(2)}) copy-start(bf16[256,1408]{1,0:T(8,128)(2,1)} %constant.27.clone.up_cols) | copy-start | bytes 2162692
  24.4 13.8 %copy-start.7 = (bf16[1408,128]{1,0:T(8,128)(2,1)S(1)}, bf16[1408,128]{1,0:T(8,128)(2,1)}, u32[]{:S(2)}) copy-start(bf16[1408,128]{1,0:T(8,128)(2,1)} %constant.28.clone.pool_cols) | copy-start | bytes 1081348
  24.5 13.8 %copy-start.16 = (bf16[8,192]{1,0:T(8,128)(2,1)S(1)}, bf16[8,192]{1,0:T(8,128)(2,1)}, u32[]{:S(2)}) copy-start(bf16[8,192]{1,0:T(8,128)(2,1)} %constant.30.clone.pool_rows) | copy-start | bytes 9220
  25.0 13.3 %copy-start.13 = (bf16[96,32]{1,0:T(8,128)(2,1)S(1)}, bf16[96,32]{1,0:T(8,128)(2,1)}, u32[]{:S(2)}) copy-start(bf16[96,32]{1,0:T(8,128)(2,1)} %constant.29.clone.up_rows) | copy-start | bytes 18436
  25.0 13.3 %collective-permute-start.6 = (f32[2,16,256]{2,1,0:T(8,128)S(1)}, f32[2,16,256]{2,1,0:T(8,128)S(1)}, u32[]{:S(2)}, u32[]{:S(2)}) collective-permute-start(f32[2,16,256]{2,1,0:T(8,128)S(1)} %get-tuple-element.40), channel_id=1, source_target_pairs={{0,64},{1,65},{2,66},{3,67},{4,68},{5,69},{6,70},{7,71},{8,72},{9,... | collective-permute-start | bytes 98312 | tf_op jit(solution)/shard_map/ppermute | solution.py:384
  38.3 18.0 %collective-permute-start.7 = (f32[8,128]{1,0:T(8,128)S(1)}, f32[8,128]{1,0:T(8,128)S(1)}, u32[]{:S(2)}, u32[]{:S(2)}) collective-permute-start(f32[8,128]{1,0:T(8,128)S(1)} %get-tuple-element.54), channel_id=1, source_target_pairs={{0,64},{1,65},{2,66},{3,67},{4,68},{5,69},{6,70},{7,71},{8,72},{9,... | collective-permute-start | bytes 12296 | tf_op jit(solution)/shard_map/ppermute | solution.py:384
where the time goes:
time: 57.5 us; the launch traced here: 57 us
  starting transfers between devices  36.4 us (63%)
  local copies, waits for them, and re-layouts  10.2 us (18%)
  waiting for transfers between devices  8.94 us (16%)
  other arithmetic  0.68 us (1%)
  Pallas kernels  0.59 us (1%)
    ppermute x8, starting transfers between devices, moved(): return lax.ppermute(array, ('comp', 'gy', 'gx'), pairs)  36.4 us
    unnamed x38, local copies, waits for them, and re-layouts  9.33 us
    ppermute x8, waiting for transfers between devices, moved(): return lax.ppermute(array, ('comp', 'gy', 'gx'), pairs)  8.94 us
  transfers between devices with their start and end apart: 8, of which 4 were waited for; matrix products, arithmetic and copies ran while one was open for 0% of the time, Pallas kernels for 0%

commit v1 on v0

--- a/solution.py
+++ b/solution.py
@@ -15,6 +15,8 @@
 STRIPS = 12
 TILES = 11
 WIDE = TILES * 128
+CHUNKS = 1
+NW = 16
 FIELDS = 5
 BF = jnp.bfloat16
 F32 = jnp.float32
@@ -36,14 +38,11 @@
     row = np.where(fine < ROWS, fine // AGG, np.where(fine < ROWS + 8, 8, 15))
     up_rows = (row[:, None] == np.arange(16)[None]).astype(np.float32)
     pool_rows = up_rows[:, :8].T * (fine < ROWS)[None]
-    own_rows = (np.arange(ROWS)[:, None] // AGG == np.arange(8)[None]).astype(np.float32)
     return dict(
         up_cols=jnp.asarray(up_cols, BF),
         pool_cols=jnp.asarray(pool_cols, BF),
         up_rows=jnp.asarray(np.concatenate([up_rows, up_rows], 1), BF),
         pool_rows=jnp.asarray(np.concatenate([pool_rows, pool_rows], 1), BF),
-        own_up=jnp.asarray(np.concatenate([own_rows, own_rows], 1), BF),
-        own_pool=jnp.asarray(np.concatenate([own_rows.T, own_rows.T], 1), BF),
     )
 
 
@@ -73,24 +72,42 @@
     return slice(t * 128, (t + 1) * 128)
 
 
+def within(shape, fine_axis):
+    fine = lax.broadcasted_iota(jnp.int32, shape, fine_axis)
+    first = AGG * lax.broadcasted_iota(jnp.int32, shape, 1 - fine_axis)
+    return jnp.where((fine >= first) & (fine < first + AGG), 1.0, 0.0).astype(BF)
+
+
 def pack_kernel(
-    water, soil, etab, stab, terrain, head, cond, mask, code, pool_cols, up_cols, own_up, own_pool,
-    gxl, gxr, main_up, main_down, gyu, gyd, keff_out, ew_out, sw_out, square,
+    water_in, soil_in, weight_in, etab_in, stab_in, terrain_in, head_in, cond_in, mask_in, code_in,
+    gxl, gxr, main_up, main_down, gyu, gyd, water, soil, weight, keff, head, code, ew, sw,
+    square, tabs, terrain, mask, code_int, sems,
 ):
     group = lax.axis_index("comp")
 
     @pl.when(group == 0)
     def _():
+        loads = [
+            pltpu.make_async_copy(water_in, water, sems.at[0]),
+            pltpu.make_async_copy(soil_in, soil, sems.at[1]),
+            pltpu.make_async_copy(weight_in, tabs.at[0], sems.at[2]),
+        ]
+        for load in loads:
+            load.start()
+        gxl[16:40] = jnp.zeros((24, 128), F32)
+        gxr[16:40] = jnp.zeros((24, 128), F32)
+        square[16:128] = jnp.zeros((112, 128), F32)
+        for load in loads:
+            load.wait()
+        square[0:8] = soil[...]
+        square[8:9, 0:LEV] = tabs[0]
+        turned = square[...].T
+        gxl[8:16] = turned[0:8]
+        gxr[8:16] = turned[120:128]
+        weight[...] = jnp.broadcast_to(turned[0:LEV, 8:9], (LEV, 128))
         square[...] = water[...].T
         gxl[0:8] = square[0:8]
         gxr[0:8] = square[120:128]
-        square[0:8] = soil[...]
-        square[8:128] = jnp.zeros((120, 128), F32)
-        turned = square[...].T
-        gxl[8:16] = turned[0:8]
-        gxr[8:16] = turned[120:128]
-        gxl[16:40] = jnp.zeros((24, 128), F32)
-        gxr[16:40] = jnp.zeros((24, 128), F32)
         for j in range(3):
             for h in range(2):
                 at = j * 16 + h * 8
@@ -101,39 +118,63 @@
 
     @pl.when(group == 1)
     def _():
-        ebig = jnp.broadcast_to(etab[...], (8, 128))
-        sbig = jnp.broadcast_to(stab[...], (8, 128))
-        for r in range(0, ROWS, 8):
-            for t in range(10):
-                at = terrain[r : r + 8, cut(t)]
-                ew_out[r : r + 8, cut(t)] = jnp.take_along_axis(ebig, at, axis=1)
-                sw_out[r : r + 8, cut(t)] = jnp.take_along_axis(sbig, at, axis=1)
-        for out in (ew_out, sw_out):
+        load_tabs = [
+            pltpu.make_async_copy(etab_in, tabs.at[1], sems.at[0]),
+            pltpu.make_async_copy(stab_in, tabs.at[2], sems.at[1]),
+        ]
+        for load in load_tabs:
+            load.start()
+        loads = []
+        for i, (source, target) in enumerate(
+            ((terrain_in, terrain), (cond_in, keff), (mask_in, mask), (head_in, head), (code_in, code_int))
+        ):
+            parts = []
+            for j in range(CHUNKS):
+                rows = pl.ds(j * (ROWS // CHUNKS), ROWS // CHUNKS)
+                parts.append(pltpu.make_async_copy(source.at[rows], target.at[rows], sems.at[2 + i * CHUNKS + j]))
+                parts[-1].start()
+            loads.append(parts)
+
+        def ready(i):
+            for part in loads[i]:
+                part.wait()
+
+        pool_cols = within((COLS, 128), 0)
+        up_cols = within((128, COLS), 1)
+        up_rows, pool_rows = within((ROWS, 8), 0), within((8, ROWS), 1)
+        for load in load_tabs:
+            load.wait()
+        ready(0)
+        for i, out in ((1, ew), (2, sw)):
+            big = jnp.concatenate([jnp.broadcast_to(tabs[i], (8, NW))] * (128 // NW), axis=1)
+            for r in range(0, ROWS, 8):
+                for t in range(10):
+                    out[r : r + 8, cut(t)] = jnp.take_along_axis(big, terrain[r : r + 8, cut(t)], axis=1)
+        for out in (ew, sw):
             high, low = split(out[...])
-            part = dot(high, pool_cols[0:COLS]) + dot(low, pool_cols[0:COLS])
+            part = dot(high, pool_cols) + dot(low, pool_cols)
             high, low = split(part)
-            total = dot(own_pool[...], jnp.concatenate([high, low], axis=0))
+            total = dot(pool_rows, high) + dot(pool_rows, low)
             high, low = split(float(AGG * AGG) / total)
-            wide = dot(jnp.concatenate([high, low], axis=0), up_cols[0:128, 0:COLS]).astype(BF)
-            out[...] = out[...] * dot(own_up[...], wide)
-        keff_out[...] = cond[...] * mask[...].astype(F32)
-        fields = (
-            lambda r, c: keff_out[r, c],
-            lambda r, c: head[r, c],
-            lambda r, c: code[r, c].astype(F32),
-            lambda r, c: ew_out[r, c],
-            lambda r, c: sw_out[r, c],
-        )
+            wide_high, wide_low = dot(high, up_cols).astype(BF), dot(low, up_cols).astype(BF)
+            out[...] = out[...] * (dot(up_rows, wide_high) + dot(up_rows, wide_low))
+        ready(1)
+        ready(2)
+        keff[...] = keff[...] * mask[...].astype(F32)
+        ready(3)
+        ready(4)
+        code[...] = code_int[...].astype(F32)
+        fields = (keff, head, code, ew, sw)
         for f, field in enumerate(fields):
             for t in range(10):
                 at = f * 80 + t * 8
-                gyu[at : at + 8] = field(slice(0, 8), cut(t))
-                gyd[at : at + 8] = field(slice(ROWS - 8, ROWS), cut(t))
+                gyu[at : at + 8] = field[0:8, cut(t)]
+                gyd[at : at + 8] = field[ROWS - 8 : ROWS, cut(t)]
         lane = lax.broadcasted_iota(jnp.int32, (ROWS, 128), 1)
         edges = jnp.zeros((ROWS, 128), F32)
         for f, field in enumerate(fields):
-            first = field(slice(0, ROWS), cut(0))
-            last = field(slice(0, ROWS), cut(9))
+            first = field[:, cut(0)]
+            last = field[:, cut(9)]
             first = first if f == 0 else pltpu.roll(first, 8 * f, 1)
             last = pltpu.roll(last, (64 + 8 * f - 120) % 128, 1)
             edges = jnp.where(lane // 8 == f, first, edges)
@@ -145,17 +186,20 @@
         gxr[...] = square[64:104]
 
 
-def middle_kernel(
-    water, soil, weight, keff, head, code, ew, sw, from_left, from_right, from_up, from_down, rows_up, rows_down,
-    coarse, water_out, a_e, a_w, a_n, a_s, a_c, m_e, m_w, m_n, m_s, m_c, head_out, ew_out, sw_out,
-    square, side, nat, kring, cring,
-):
-    group = lax.axis_index("comp")
+def edges_of_grid():
     gy, gx = lax.axis_index("gy"), lax.axis_index("gx")
     has_up = (gy > 0).astype(F32)
     has_down = (gy < lax.axis_size("gy") - 1).astype(F32)
     has_left = (gx > 0).astype(F32)
     has_right = (gx < lax.axis_size("gx") - 1).astype(F32)
+    return has_up, has_down, has_left, has_right
+
+
+def land_kernel(
+    water, soil, weight, from_left, from_right, from_up, from_down, coarse, water_out, square, side,
+):
+    group = lax.axis_index("comp")
+    has_up, has_down, has_left, has_right = edges_of_grid()
 
     @pl.when(group == 0)
     def _():
@@ -215,7 +259,7 @@
         twice = sweep(once, 2, 12)
         for j in range(8):
             water_out[j : j + 1] = twice[3 + j][0:1, 0:128]
-        level_weight = jnp.broadcast_to(weight[...], (LEV, 256))
+        level_weight = jnp.concatenate([weight[...]] * 2, axis=1)
         rain = {q: jnp.sum(level_weight * twice[q] * twice[q], axis=0, keepdims=True) for q in twice}
         blank = jnp.zeros((6, 256), F32)
         rain = jnp.concatenate([rain[3 + j] for j in range(8)] + [rain[11], blank, rain[2]], axis=0)
@@ -231,6 +275,15 @@
         coarse[0] = rain * moist * moist / (moist * moist + half_point)
         coarse[1] = moist
 
+
+def prepare_kernel(
+    keff, head, code, ew, sw, from_left, from_right, from_up, from_down, rows_up, rows_down, after,
+    a_e, a_w, a_n, a_s, a_c, m_e, m_w, m_n, m_s, m_c, head_out, ew_out, sw_out,
+    square, side, nat, kring, cring,
+):
+    group = lax.axis_index("comp")
+    has_up, has_down, has_left, has_right = edges_of_grid()
+
     @pl.when(group == 1)
     def _():
         lane128 = lax.broadcasted_iota(jnp.int32, (40, 128), 1)
@@ -242,22 +295,16 @@
         square[...] = jnp.zeros((128, 128), F32)
         square[0:40] = column(from_right[...], from_down[40:80], from_up[40:80]) * has_right
         square[64:104] = column(from_left[...], from_down[0:40], from_up[0:40]) * has_left
-        side[0] = square[...].T
-        own = (
-            lambda c: keff[:, c],
-            lambda c: head[:, c],
-            lambda c: code[:, c].astype(F32),
-            lambda c: ew[:, c],
-            lambda c: sw[:, c],
-        )
+        side[...] = square[...].T
+        own = (keff, head, code, ew, sw)
         lane = lax.broadcasted_iota(jnp.int32, (96, 128), 1)
         for f in range(FIELDS):
             for t in range(10):
                 at = f * 80 + t * 8
-                nat[t, 0:ROWS] = own[f](cut(t))
+                nat[t, 0:ROWS] = own[f][:, cut(t)]
                 nat[t, ROWS : ROWS + 8] = rows_down[at : at + 8] * has_down
                 nat[t, ROWS + 8 : ROWS + 16] = rows_up[at : at + 8] * has_up
-            columns = side[0, 0:96]
+            columns = side[0:96]
             right = columns if f == 0 else pltpu.roll(columns, (-8 * f) % 128, 1)
             left = pltpu.roll(columns, 120 - 64 - 8 * f, 1)
             nat[10] = jnp.where(lane < 8, right, jnp.where(lane >= 120, left, 0.0))
@@ -335,29 +382,36 @@
         close(store_a)
 
         def substep(pond, store, new_pond, new_store):
-            def strip(k, carry):
-                lane = lanes()
-                p = [pond[k + 1, :, cut(t)] for t in range(TILES)]
-                s = [store[k + 1, :, cut(t)] for t in range(TILES)]
-                q = [x * x for x in s]
-                p_w, p_e = beside(p, lane)
-                q_w, q_e = beside(q, lane)
+            lane = lanes()
+            first, last = lane == 0, lane == 127
+            for k in range(STRIPS):
+                p, s = pond[k + 1, :, cut(0)], store[k + 1, :, cut(0)]
+                q = s * s
+                p_left, q_left = pltpu.roll(p, 127, 1), pltpu.roll(q, 127, 1)
+                s_r = store[k + 1, :, cut(TILES - 1)]
+                p_before = pltpu.roll(pond[k + 1, :, cut(TILES - 1)], 1, 1)
+                q_before = pltpu.roll(s_r * s_r, 1, 1)
                 for t in range(TILES):
-                    c = cut(t)
+                    c, after = cut(t), cut((t + 1) % TILES)
+                    p_next, s_next = pond[k + 1, :, after], store[k + 1, :, after]
+                    q_next = s_next * s_next
+                    p_right, q_right = pltpu.roll(p, 1, 1), pltpu.roll(q, 1, 1)
+                    p_next_left, q_next_left = pltpu.roll(p_next, 127, 1), pltpu.roll(q_next, 127, 1)
+                    p_w, p_e = jnp.where(first, p_before, p_right), jnp.where(last, p_next_left, p_left)
+                    q_w, q_e = jnp.where(first, q_before, q_right), jnp.where(last, q_next_left, q_left)
                     s_n, s_s = store[k, :, c], store[k + 2, :, c]
-                    below = 1.0 + s[t]
-                    guess = pl.reciprocal(below, approx=True)
+                    below = 1.0 + s
+                    guess = pltpu.reciprocal(below, approx=True)
                     guess = guess * (2.0 - below * guess)
-                    soaked = infiltration_rate * p[t] * guess
+                    soaked = infiltration_rate * p * guess
                     flow = a_n[k, :, c] * pond[k, :, c] + a_s[k, :, c] * pond[k + 2, :, c]
-                    flow = flow + (a_w[k, :, c] * p_w[t] + a_e[k, :, c] * p_e[t])
-                    new_pond[k + 1, :, c] = a_c[k, :, c] * p[t] + flow - soaked
+                    flow = flow + (a_w[k, :, c] * p_w + a_e[k, :, c] * p_e)
+                    new_pond[k + 1, :, c] = a_c[k, :, c] * p + flow - soaked
                     inflow = m_n[k, :, c] * (s_n * s_n) + m_s[k, :, c] * (s_s * s_s)
-                    inflow = inflow + (m_w[k, :, c] * q_w[t] + m_e[k, :, c] * q_e[t])
-                    new_store[k + 1, :, c] = s[t] + soaked - m_c[k, :, c] * q[t] + inflow
-                return carry
-
-            lax.fori_loop(0, STRIPS, strip, 0)
+                    inflow = inflow + (m_w[k, :, c] * q_w + m_e[k, :, c] * q_e)
+                    new_store[k + 1, :, c] = s + soaked - m_c[k, :, c] * q + inflow
+                    p, s, q, p_left, q_left = p_next, s_next, q_next, p_next_left, q_next_left
+                    p_before, q_before = p_right, q_right
             close(new_pond)
             close(new_store)
 
@@ -403,49 +457,66 @@
     shape = tuple(lax.axis_size(axis) for axis in ("comp", "gy", "gx"))
     group = lax.axis_index("comp")
     m = tables()
-    water = column_water[0].reshape(128, 128)
-    soil = land_soil[0]
-    etab = jnp.pad(excess_weight, (0, 112))[None]
-    stab = jnp.pad(soil_weight, (0, 112))[None]
     params = pltpu.CompilerParams(vmem_limit_bytes=32 * 1024 * 1024)
-    gxl, gxr, main_up, main_down, gyu, gyd, keff, ew, sw = pl.pallas_call(
+    arguments = (
+        column_water[0].reshape(128, 128), land_soil[0], level_weight[None], excess_weight[None], soil_weight[None],
+        terrain_class, surface_head[0], conductivity[0], active_mask[0], flow_code[0],
+    )
+    hbm = pl.BlockSpec(memory_space=pltpu.HBM)
+    fine = f32(ROWS, COLS)
+    fine_int = pltpu.VMEM((ROWS, COLS), jnp.int32)
+    gxl, gxr, main_up, main_down, gyu, gyd, water, soil, weight, keff, head, code, ew, sw = pl.pallas_call(
         pack_kernel,
-        out_shape=[f32(40, 128)] * 2 + [f32(56, 128)] * 2 + [f32(400, 128)] * 2 + [f32(ROWS, COLS)] * 3,
-        scratch_shapes=[pltpu.VMEM((128, 128), F32)],
+        in_specs=[hbm] * 10,
+        out_shape=[f32(40, 128)] * 2
+        + [f32(56, 128)] * 2
+        + [f32(400, 128)] * 2
+        + [f32(128, 128), f32(8, 128), f32(LEV, 128)]
+        + [fine] * 5,
+        scratch_shapes=[
+            pltpu.VMEM((128, 128), F32),
+            pltpu.VMEM((3, 1, NW), F32),
+            fine_int,
+            fine_int,
+            fine_int,
+            pltpu.SemaphoreType.DMA((2 + 5 * CHUNKS,)),
+        ],
         compiler_params=params,
         name="pack",
-    )(
-        water, soil, etab, stab, terrain_class, surface_head[0], conductivity[0], active_mask[0], flow_code[0],
-        m["pool_cols"], m["up_cols"], m["own_up"], m["own_pool"],
-    )
+    )(*(pltpu.with_memory_space_constraint(array, pltpu.HBM) for array in arguments))
     from_left = moved(gxr, shape, lambda g, y, x: (g, y, x + 1))
     from_right = moved(gxl, shape, lambda g, y, x: (g, y, x - 1))
-    rows_up = moved(gyd, shape, lambda g, y, x: (g, y + g, x))
-    rows_down = moved(gyu, shape, lambda g, y, x: (g, y - g, x))
-    land = jnp.concatenate([from_left[:16], from_right[:16]])
-    route = jnp.concatenate([from_left, from_right, jnp.zeros((8, 128), F32)])
-    send_up = jnp.where(group == 0, jnp.concatenate([land, main_up]), route)
-    send_down = jnp.where(group == 0, jnp.concatenate([land, main_down]), route)
-    from_up = moved(send_down, shape, lambda g, y, x: (g, y + 1, x))
-    from_down = moved(send_up, shape, lambda g, y, x: (g, y - 1, x))
+    rows_up = moved(gyd, shape, lambda g, y, x: (g, y + 1, x) if g else (g, y, x ^ 1))
+    rows_down = moved(gyu, shape, lambda g, y, x: (g, y - 1, x) if g else (g, y, x ^ 1))
+    land = [from_left[:16], from_right[:16]]
+    land_up = moved(jnp.concatenate(land + [main_down]), shape, lambda g, y, x: (g, y, x ^ 1) if g else (g, y + 1, x))
+    land_down = moved(jnp.concatenate(land + [main_up]), shape, lambda g, y, x: (g, y, x ^ 1) if g else (g, y - 1, x))
+    route = jnp.concatenate([from_left, from_right])
+    route_up = moved(route, shape, lambda g, y, x: (g, y + 1, x) if g else (g, y, x ^ 1))
+    route_down = moved(route, shape, lambda g, y, x: (g, y - 1, x) if g else (g, y, x ^ 1))
+    coarse, water_top = pl.pallas_call(
+        land_kernel,
+        out_shape=[f32(2, 16, 256), f32(8, 128)],
+        scratch_shapes=[pltpu.VMEM((128, 128), F32), pltpu.VMEM((3, 128, 128), F32)],
+        compiler_params=params,
+        name="land",
+    )(water, soil, weight, from_left, from_right, land_up, land_down)
+    arrived = moved(coarse, shape, lambda g, y, x: (1 - g, y, x))
     strips = f32(STRIPS, 8, WIDE)
-    coarse, water_top, *prepared = pl.pallas_call(
-        middle_kernel,
-        out_shape=[f32(2, 16, 256), f32(8, 128)] + [strips] * 13,
+    ring = pltpu.VMEM((STRIPS + 2, 8, WIDE), F32)
+    prepared = pl.pallas_call(
+        prepare_kernel,
+        out_shape=[strips] * 13,
         scratch_shapes=[
             pltpu.VMEM((128, 128), F32),
-            pltpu.VMEM((3, 128, 128), F32),
+            pltpu.VMEM((128, 128), F32),
             pltpu.VMEM((TILES, 96, 128), F32),
-            pltpu.VMEM((STRIPS + 2, 8, WIDE), F32),
-            pltpu.VMEM((STRIPS + 2, 8, WIDE), F32),
+            ring,
+            ring,
         ],
         compiler_params=params,
-        name="middle",
-    )(
-        water, soil, level_weight[:, None], keff, surface_head[0], flow_code[0], ew, sw,
-        from_left, from_right, from_up, from_down, rows_up, rows_down,
-    )
-    arrived = moved(coarse, shape, lambda g, y, x: (1 - g, y, x))
+        name="prepare",
+    )(keff, head, code, ew, sw, from_left, from_right, route_up, route_down, rows_up, rows_down, water_top)
     ring = pltpu.VMEM((STRIPS + 2, 8, WIDE), F32)
     ponded, stored = pl.pallas_call(
         route_kernel,

time: 57.5 us -> 37.9 us (0.66)
  starting transfers between devices: 36.4 us -> 24.7 us
  local copies, waits for them, and re-layouts: 10.2 us -> 0.04 us
  waiting for transfers between devices: 8.94 us -> 10.7 us
  Pallas kernels: 0.59 us -> 1.53 us
    ppermute x8 -> x10, starting transfers between devices: 36.4 us -> 24.7 us  [moved(): return lax.ppermute(array, ('comp', 'gy', 'gx'), pairs)]
    unnamed x38 -> x9, local copies, waits for them, and re-layouts: 9.33 us -> 0.03 us
    ppermute x8 -> x10, waiting for transfers between devices: 8.94 us -> 10.7 us  [moved(): return lax.ppermute(array, ('comp', 'gy', 'gx'), pairs)]
    pallas_call x2 -> x3, Pallas kernels: 0.57 us -> 1.51 us  [the longest x1 1.05 us: per_device(): pl.pallas_call(pack_kernel, in_specs=[hbm] * 10, out_shape=[f32(40, 128)]...]
    broadcast_in_dim x3 -> x0, local copies, waits for them, and re-layouts: 0.77 us -> none  [the longest x1 0.69 us: per_device(): stab = jnp.pad(soil_weight, (0, 112))[None]]
  transfers between devices with their start and end apart: 8 -> 10, of which waited for: 4 -> 6; matrix products, arithmetic and copies ran while one was open for 0% -> 0% of each run, Pallas kernels for 0% -> 1%
where the time goes in v1:
time: 37.9 us; the launch traced here: 37.7 us
  starting transfers between devices  24.7 us (65%)
  waiting for transfers between devices  10.7 us (28%)
  Pallas kernels  1.53 us (4%)
  other arithmetic  0.62 us (2%)
    ppermute x10, starting transfers between devices, moved(): return lax.ppermute(array, ('comp', 'gy', 'gx'), pairs)  24.7 us
    ppermute x10, waiting for transfers between devices, moved(): return lax.ppermute(array, ('comp', 'gy', 'gx'), pairs)  10.7 us
    pallas_call x1, Pallas kernels, per_device(): pl.pallas_call(pack_kernel, in_specs=[hbm] * 10, out_shape=[f32(40, 128)]...  1.05 us
  transfers between devices with their start and end apart: 10, of which 6 were waited for; matrix products, arithmetic and copies ran while one was open for 0% of the time, Pallas kernels for 1%

profile of v1, /device:TPU:0, one launch (start us, length us, event | category | flops | bytes accessed | tf_op | source)
XLA Modules:
  0.0 37.7 jit_solution(8282704119249002514)
XLA Ops:
  0.0 1.1 %pack.1 = (f32[40,128]{1,0:T(8,128)S(1)}, f32[40,128]{1,0:T(8,128)S(1)}, f32[56,128]{1,0:T(8,128)S(1)}, f32[56,128]{1,0:T(8,128)S(1)}, f32[400,128]{1,0:T(8,128)...) custom-call(f32[128,128]{1,0:T(8,128)} %bitcast.15, ...), custom_call_target="tpu_custom_call" | custom-call | tf_op jit(solution)/shard_map/pack/pallas_call | solution.py:468
  1.1 2.5 %collective-permute-start.1 = (f32[40,128]{1,0:T(8,128)S(1)}, f32[40,128]{1,0:T(8,128)S(1)}, u32[]{:S(2)}, u32[]{:S(2)}) collective-permute-start(f32[40,128]{1,0:T(8,128)S(1)} %get-tuple-element.40), channel_id=1, source_target_pairs={{0,7},{1,0},{2,1},{3,2},{4,3},{5,4},{6,5},{7,6},{8,15},{9,8},{10,9... | collective-permute-start | bytes 61448 | tf_op jit(solution)/shard_map/ppermute | solution.py:438
  3.6 0.0 collective-permute-start
  3.6 0.0 collective-permute-start.7
  3.6 0.5 %collective-permute-start.8 = (f32[400,128]{1,0:T(8,128)S(1)}, f32[400,128]{1,0:T(8,128)S(1)}, u32[]{:S(2)}, u32[]{:S(2)}) collective-permute-start(f32[400,128]{1,0:T(8,128)S(1)} %get-tuple-element.50), channel_id=1, source_target_pairs={{0,1},{1,0},{2,3},{3,2},{4,5},{5,4},{6,7},{7,6},{8,9},{9,8},{10,11... | collective-permute-start | bytes 614408 | tf_op jit(solution)/shard_map/ppermute | solution.py:438
  4.1 1.0 %collective-permute-done.1.from_right = f32[40,128]{1,0:T(8,128)S(1)} collective-permute-done((f32[40,128]{1,0:T(8,128)S(1)}, f32[40,128]{1,0:T(8,128)S(1)}, u32[]{:S(2)}, u32[]{:S(2)}) %collective-permute-start.1) | collective-permute-done | bytes 20512 | tf_op jit(solution)/shard_map/ppermute | solution.py:438
  5.1 2.9 %collective-permute-done.from_left = f32[40,128]{1,0:T(8,128)S(1)} collective-permute-done((f32[40,128]{1,0:T(8,128)S(1)}, f32[40,128]{1,0:T(8,128)S(1)}, u32[]{:S(2)}, u32[]{:S(2)}) %collective-permute-start) | collective-permute-done | bytes 20512 | tf_op jit(solution)/shard_map/ppermute | solution.py:438
  8.0 2.0 %collective-permute-start.2 = (f32[88,128]{1,0:T(8,128)S(1)}, f32[88,128]{1,0:T(8,128)S(1)}, u32[]{:S(2)}, u32[]{:S(2)}) collective-permute-start(f32[88,128]{1,0:T(8,128)S(1)} %get-tuple-element.68), channel_id=1, source_target_pairs={{0,8},{1,9},{2,10},{3,11},{4,12},{5,13},{6,14},{7,15},{8,16},{9,17... | collective-permute-start | bytes 135176 | tf_op jit(solution)/shard_map/ppermute | solution.py:438
  10.0 2.3 %collective-permute-start.3 = (f32[88,128]{1,0:T(8,128)S(1)}, f32[88,128]{1,0:T(8,128)S(1)}, u32[]{:S(2)}, u32[]{:S(2)}) collective-permute-start(f32[88,128]{1,0:T(8,128)S(1)} %get-tuple-element.67), channel_id=1, source_target_pairs={{0,56},{1,57},{2,58},{3,59},{4,60},{5,61},{6,62},{7,63},{8,0},{9,1... | collective-permute-start | bytes 135176 | tf_op jit(solution)/shard_map/ppermute | solution.py:438
  12.3 0.0 collective-permute-start.5
  12.3 2.1 %collective-permute-done.2.from_up = f32[88,128]{1,0:T(8,128)S(1)} collective-permute-done((f32[88,128]{1,0:T(8,128)S(1)}, f32[88,128]{1,0:T(8,128)S(1)}, u32[]{:S(2)}, u32[]{:S(2)}) %collective-permute-start.2) | collective-permute-done | bytes 45088 | tf_op jit(solution)/shard_map/ppermute | solution.py:438
  14.4 0.0 collective-permute-start.6
  14.4 0.2 collective-permute-done.3.from_down
  14.6 0.4 %land.1 = (f32[2,16,256]{2,1,0:T(8,128)S(1)}, f32[8,128]{1,0:T(8,128)S(1)}) custom-call(f32[128,128]{1,0:T(8,128)S(1)} %get-tuple-element.36.water, f32[8,128]{1,0:T(8,128)S(1)} %get-tuple-element.37.soil, f32[16,128]{1,0:T(8,128)S(1)} %get-tuple-element.38.weight, f32[40,128]{1,0:T(8,128)S(1)} %collective-permute-done.from_left, ...), custom_call_target="tpu_custom_call" | custom-call | tf_op jit(solution)/shard_map/land/pallas_call | solution.py:497
  15.0 4.3 %collective-permute-start.4 = (f32[2,16,256]{2,1,0:T(8,128)S(1)}, f32[2,16,256]{2,1,0:T(8,128)S(1)}, u32[]{:S(2)}, u32[]{:S(2)}) collective-permute-start(f32[2,16,256]{2,1,0:T(8,128)S(1)} %get-tuple-element.43), channel_id=1, source_target_pairs={{0,64},{1,65},{2,66},{3,67},{4,68},{5,69},{6,70},{7,71},{8,72},{9,... | collective-permute-start | bytes 98312 | tf_op jit(solution)/shard_map/ppermute | solution.py:438
  19.3 0.0 collective-permute-done.5.from_up
  19.3 0.0 collective-permute-done.6.from_down
  19.3 0.0 collective-permute-done.7.rows_up
  19.3 0.0 collective-permute-done.8.rows_down
  19.3 0.0 copy-start
  19.3 0.0 copy-start.1
  19.3 0.0 copy-start.3
  19.4 0.0 copy-start.2
  19.4 3.0 %collective-permute-done.4.coarse = f32[2,16,256]{2,1,0:T(8,128)S(1)} collective-permute-done((f32[2,16,256]{2,1,0:T(8,128)S(1)}, f32[2,16,256]{2,1,0:T(8,128)S(1)}, u32[]{:S(2)}, u32[]{:S(2)}) %collective-permute-start.4) | collective-permute-done | bytes 32800 | tf_op jit(solution)/shard_map/ppermute | solution.py:438
  22.4 0.0 copy-done
  22.4 0.0 copy-done.1
  22.4 0.0 copy-done.3
  22.4 0.0 copy-done.2
  22.4 13.1 %collective-permute-start.9 = (f32[8,128]{1,0:T(8,128)S(1)}, f32[8,128]{1,0:T(8,128)S(1)}, u32[]{:S(2)}, u32[]{:S(2)}) collective-permute-start(f32[8,128]{1,0:T(8,128)S(1)} %get-tuple-element.65), channel_id=1, source_target_pairs={{0,64},{1,65},{2,66},{3,67},{4,68},{5,69},{6,70},{7,71},{8,72},{9,... | collective-permute-start | bytes 12296 | tf_op jit(solution)/shard_map/ppermute | solution.py:438
  35.5 1.6 %collective-permute-done.9 = f32[8,128]{1,0:T(8,128)S(1)} collective-permute-done((f32[8,128]{1,0:T(8,128)S(1)}, f32[8,128]{1,0:T(8,128)S(1)}, u32[]{:S(2)}, u32[]{:S(2)}) %collective-permute-start.9) | collective-permute-done | bytes 4128 | tf_op jit(solution)/shard_map/ppermute | solution.py:438
  37.1 0.6 %fusion.4 = f32[1,8,128]{2,1,0:T(8,128)} fusion(f32[8,128]{1,0:T(8,128)S(1)} %get-tuple-element.66, f32[8,128]{1,0:T(8,128)S(1)} %collective-permute-done.9, f32[8,128]{1,0:T(8,128)S(1)} %get-tuple-element.51.after, pred[]{:T(512)S(6)} %eq.3), kind=kLoop, calls=%fused_computation.9 | loop fusion | flops 5120 | bytes 16385 | tf_op jit(solution)/shard_map/broadcast_in_dim | solution.py:530
  (7 shorter events, 0.1 us)
Async XLA Ops:
  1.1 4.0 %collective-permute-start.1 = (f32[40,128]{1,0:T(8,128)S(1)}, f32[40,128]{1,0:T(8,128)S(1)}, u32[]{:S(2)}, u32[]{:S(2)}) collective-permute-start(f32[40,128]{1,0:T(8,128)S(1)} %get-tuple-element.40), channel_id=1, source_target_pairs={{0,7},{1,0},{2,1},{3,2},{4,3},{5,4},{6,5},{7,6},{8,15},{9,8},{10,9... | collective-permute-start | bytes 61448 | tf_op jit(solution)/shard_map/ppermute | solution.py:438
  3.6 4.4 %collective-permute-start = (f32[40,128]{1,0:T(8,128)S(1)}, f32[40,128]{1,0:T(8,128)S(1)}, u32[]{:S(2)}, u32[]{:S(2)}) collective-permute-start(f32[40,128]{1,0:T(8,128)S(1)} %get-tuple-element.39), channel_id=1, source_target_pairs={{0,1},{1,2},{2,3},{3,4},{4,5},{5,6},{6,7},{7,0},{8,9},{9,10},{10,1... | collective-permute-start | bytes 61448 | tf_op jit(solution)/shard_map/ppermute | solution.py:438
  3.6 15.6 %collective-permute-start.7 = (f32[400,128]{1,0:T(8,128)S(1)}, f32[400,128]{1,0:T(8,128)S(1)}, u32[]{:S(2)}, u32[]{:S(2)}) collective-permute-start(f32[400,128]{1,0:T(8,128)S(1)} %get-tuple-element.49), channel_id=1, source_target_pairs={{0,1},{1,0},{2,3},{3,2},{4,5},{5,4},{6,7},{7,6},{8,9},{9,8},{10,11... | collective-permute-start | bytes 614408 | tf_op jit(solution)/shard_map/ppermute | solution.py:438
  3.6 15.6 %collective-permute-start.8 = (f32[400,128]{1,0:T(8,128)S(1)}, f32[400,128]{1,0:T(8,128)S(1)}, u32[]{:S(2)}, u32[]{:S(2)}) collective-permute-start(f32[400,128]{1,0:T(8,128)S(1)} %get-tuple-element.50), channel_id=1, source_target_pairs={{0,1},{1,0},{2,3},{3,2},{4,5},{5,4},{6,7},{7,6},{8,9},{9,8},{10,11... | collective-permute-start | bytes 614408 | tf_op jit(solution)/shard_map/ppermute | solution.py:438
  8.0 6.3 %collective-permute-start.2 = (f32[88,128]{1,0:T(8,128)S(1)}, f32[88,128]{1,0:T(8,128)S(1)}, u32[]{:S(2)}, u32[]{:S(2)}) collective-permute-start(f32[88,128]{1,0:T(8,128)S(1)} %get-tuple-element.68), channel_id=1, source_target_pairs={{0,8},{1,9},{2,10},{3,11},{4,12},{5,13},{6,14},{7,15},{8,16},{9,17... | collective-permute-start | bytes 135176 | tf_op jit(solution)/shard_map/ppermute | solution.py:438
  10.0 4.5 %collective-permute-start.3 = (f32[88,128]{1,0:T(8,128)S(1)}, f32[88,128]{1,0:T(8,128)S(1)}, u32[]{:S(2)}, u32[]{:S(2)}) collective-permute-start(f32[88,128]{1,0:T(8,128)S(1)} %get-tuple-element.67), channel_id=1, source_target_pairs={{0,56},{1,57},{2,58},{3,59},{4,60},{5,61},{6,62},{7,63},{8,0},{9,1... | collective-permute-start | bytes 135176 | tf_op jit(solution)/shard_map/ppermute | solution.py:438
  12.3 6.9 %collective-permute-start.5 = (f32[80,128]{1,0:T(8,128)S(1)}, f32[80,128]{1,0:T(8,128)S(1)}, u32[]{:S(2)}, u32[]{:S(2)}) collective-permute-start(f32[80,128]{1,0:T(8,128)S(1)} %constant_dynamic-update-slice_fusion), channel_id=1, source_target_pairs={{0,1},{1,0},{2,3},{3,2},{4,5},{5,4},{6,7},{7,6},{8,9},{9,8},{10,11... | collective-permute-start | bytes 122888 | tf_op jit(solution)/shard_map/ppermute | solution.py:438
  14.4 4.9 %collective-permute-start.6 = (f32[80,128]{1,0:T(8,128)S(1)}, f32[80,128]{1,0:T(8,128)S(1)}, u32[]{:S(2)}, u32[]{:S(2)}) collective-permute-start(f32[80,128]{1,0:T(8,128)S(1)} %constant_dynamic-update-slice_fusion), channel_id=1, source_target_pairs={{0,1},{1,0},{2,3},{3,2},{4,5},{5,4},{6,7},{7,6},{8,9},{9,8},{10,11... | collective-permute-start | bytes 122888 | tf_op jit(solution)/shard_map/ppermute | solution.py:438
  15.0 7.4 %collective-permute-start.4 = (f32[2,16,256]{2,1,0:T(8,128)S(1)}, f32[2,16,256]{2,1,0:T(8,128)S(1)}, u32[]{:S(2)}, u32[]{:S(2)}) collective-permute-start(f32[2,16,256]{2,1,0:T(8,128)S(1)} %get-tuple-element.43), channel_id=1, source_target_pairs={{0,64},{1,65},{2,66},{3,67},{4,68},{5,69},{6,70},{7,71},{8,72},{9,... | collective-permute-start | bytes 98312 | tf_op jit(solution)/shard_map/ppermute | solution.py:438
  19.3 3.1 %copy-start = (bf16[256,1408]{1,0:T(8,128)(2,1)S(1)}, bf16[256,1408]{1,0:T(8,128)(2,1)}, u32[]{:S(2)}) copy-start(bf16[256,1408]{1,0:T(8,128)(2,1)} %constant.20.clone.up_cols) | copy-start | bytes 2162692
  19.3 3.1 %copy-start.1 = (bf16[1408,128]{1,0:T(8,128)(2,1)S(1)}, bf16[1408,128]{1,0:T(8,128)(2,1)}, u32[]{:S(2)}) copy-start(bf16[1408,128]{1,0:T(8,128)(2,1)} %constant.21.clone.pool_cols) | copy-start | bytes 1081348
  19.3 3.1 %copy-start.3 = (bf16[8,192]{1,0:T(8,128)(2,1)S(1)}, bf16[8,192]{1,0:T(8,128)(2,1)}, u32[]{:S(2)}) copy-start(bf16[8,192]{1,0:T(8,128)(2,1)} %constant.23.clone.pool_rows) | copy-start | bytes 9220
  19.4 3.0 %copy-start.2 = (bf16[96,32]{1,0:T(8,128)(2,1)S(1)}, bf16[96,32]{1,0:T(8,128)(2,1)}, u32[]{:S(2)}) copy-start(bf16[96,32]{1,0:T(8,128)(2,1)} %constant.22.clone.up_rows) | copy-start | bytes 18436
  22.4 14.7 %collective-permute-start.9 = (f32[8,128]{1,0:T(8,128)S(1)}, f32[8,128]{1,0:T(8,128)S(1)}, u32[]{:S(2)}, u32[]{:S(2)}) collective-permute-start(f32[8,128]{1,0:T(8,128)S(1)} %get-tuple-element.65), channel_id=1, source_target_pairs={{0,64},{1,65},{2,66},{3,67},{4,68},{5,69},{6,70},{7,71},{8,72},{9,... | collective-permute-start | bytes 12296 | tf_op jit(solution)/shard_map/ppermute | solution.py:438

commit v2 on v1

--- a/solution.py
+++ b/solution.py
@@ -1,6 +1,5 @@
 import jax
 import jax.numpy as jnp
-import numpy as np
 from jax import lax
 from jax.experimental import pallas as pl
 from jax.experimental.pallas import tpu as pltpu
@@ -17,7 +16,6 @@
 WIDE = TILES * 128
 CHUNKS = 1
 NW = 16
-FIELDS = 5
 BF = jnp.bfloat16
 F32 = jnp.float32
 
@@ -28,24 +26,6 @@
 evaporation_scale = 0.5
 
 
-def tables():
-    lane = np.arange(WIDE)
-    col = np.where(lane < COLS, lane // AGG, np.where(lane < COLS + 8, 128, np.where(lane >= WIDE - 8, 255, -1)))
-    up_cols = (np.arange(256)[:, None] == col[None]).astype(np.float32)
-    pool_cols = up_cols[:128].T.copy()
-    k, s = np.meshgrid(np.arange(STRIPS), np.arange(8), indexing="ij")
-    fine = (12 * s + k).reshape(-1)
-    row = np.where(fine < ROWS, fine // AGG, np.where(fine < ROWS + 8, 8, 15))
-    up_rows = (row[:, None] == np.arange(16)[None]).astype(np.float32)
-    pool_rows = up_rows[:, :8].T * (fine < ROWS)[None]
-    return dict(
-        up_cols=jnp.asarray(up_cols, BF),
-        pool_cols=jnp.asarray(pool_cols, BF),
-        up_rows=jnp.asarray(np.concatenate([up_rows, up_rows], 1), BF),
-        pool_rows=jnp.asarray(np.concatenate([pool_rows, pool_rows], 1), BF),
-    )
-
-
 def split(x):
     high = x.astype(BF)
     return high, (x - high.astype(F32)).astype(BF)
@@ -53,6 +33,18 @@
 
 def dot(a, b):
     return jnp.dot(a, b, preferred_element_type=F32)
+
+
+def both(x):
+    return jnp.concatenate(split(x), axis=0)
+
+
+def inverse(total):
+    return float(AGG * AGG) / jnp.where(total > 0.0, total, 1.0)
+
+
+def twice(x):
+    return jnp.concatenate([x, x], axis=1)
 
 
 def lanes():
@@ -80,8 +72,8 @@
 
 def pack_kernel(
     water_in, soil_in, weight_in, etab_in, stab_in, terrain_in, head_in, cond_in, mask_in, code_in,
-    gxl, gxr, main_up, main_down, gyu, gyd, water, soil, weight, keff, head, code, ew, sw,
-    square, tabs, terrain, mask, code_int, sems,
+    gxl, gxr, main_up, main_down, gyu, gyd, water, soil, weight, tabs, terrain, keff, head, code,
+    square, mask, code_int, sems,
 ):
     group = lax.axis_index("comp")
 
@@ -122,8 +114,6 @@
             pltpu.make_async_copy(etab_in, tabs.at[1], sems.at[0]),
             pltpu.make_async_copy(stab_in, tabs.at[2], sems.at[1]),
         ]
-        for load in load_tabs:
-            load.start()
         loads = []
         for i, (source, target) in enumerate(
             ((terrain_in, terrain), (cond_in, keff), (mask_in, mask), (head_in, head), (code_in, code_int))
@@ -135,55 +125,107 @@
                 parts[-1].start()
             loads.append(parts)
 
+        for load in load_tabs:
+            load.start()
+
         def ready(i):
             for part in loads[i]:
                 part.wait()
 
-        pool_cols = within((COLS, 128), 0)
-        up_cols = within((128, COLS), 1)
-        up_rows, pool_rows = within((ROWS, 8), 0), within((8, ROWS), 1)
-        for load in load_tabs:
-            load.wait()
-        ready(0)
-        for i, out in ((1, ew), (2, sw)):
-            big = jnp.concatenate([jnp.broadcast_to(tabs[i], (8, NW))] * (128 // NW), axis=1)
-            for r in range(0, ROWS, 8):
-                for t in range(10):
-                    out[r : r + 8, cut(t)] = jnp.take_along_axis(big, terrain[r : r + 8, cut(t)], axis=1)
-        for out in (ew, sw):
-            high, low = split(out[...])
-            part = dot(high, pool_cols) + dot(low, pool_cols)
-            high, low = split(part)
-            total = dot(pool_rows, high) + dot(pool_rows, low)
-            high, low = split(float(AGG * AGG) / total)
-            wide_high, wide_low = dot(high, up_cols).astype(BF), dot(low, up_cols).astype(BF)
-            out[...] = out[...] * (dot(up_rows, wide_high) + dot(up_rows, wide_low))
         ready(1)
         ready(2)
         keff[...] = keff[...] * mask[...].astype(F32)
-        ready(3)
         ready(4)
         code[...] = code_int[...].astype(F32)
-        fields = (keff, head, code, ew, sw)
+        ready(3)
+        ready(0)
+
+        def terrain_at(r, c):
+            return terrain[r, c].astype(F32)
+
+        fields = (lambda r, c: keff[r, c], lambda r, c: head[r, c], lambda r, c: code[r, c], terrain_at)
         for f, field in enumerate(fields):
             for t in range(10):
                 at = f * 80 + t * 8
-                gyu[at : at + 8] = field[0:8, cut(t)]
-                gyd[at : at + 8] = field[ROWS - 8 : ROWS, cut(t)]
+                gyu[at : at + 8] = field(slice(0, 8), cut(t))
+                gyd[at : at + 8] = field(slice(ROWS - 8, ROWS), cut(t))
+        for t in range(10):
+            at = 320 + 2 * t
+            gyu[at : at + 2] = terrain_at(slice(8, 10), cut(t))
+            gyd[at : at + 2] = terrain_at(slice(ROWS - 10, ROWS - 8), cut(t))
+        gyu[340:344] = jnp.zeros((4, 128), F32)
+        gyd[340:344] = jnp.zeros((4, 128), F32)
         lane = lax.broadcasted_iota(jnp.int32, (ROWS, 128), 1)
         edges = jnp.zeros((ROWS, 128), F32)
         for f, field in enumerate(fields):
-            first = field[:, cut(0)]
-            last = field[:, cut(9)]
+            width = 8 if f < 3 else AGG
+            first = field(slice(0, ROWS), cut(0))
+            last = field(slice(0, ROWS), cut(9))
             first = first if f == 0 else pltpu.roll(first, 8 * f, 1)
-            last = pltpu.roll(last, (64 + 8 * f - 120) % 128, 1)
-            edges = jnp.where(lane // 8 == f, first, edges)
-            edges = jnp.where(lane // 8 == 8 + f, last, edges)
+            last = pltpu.roll(last, (64 + 8 * f + width) % 128, 1)
+            edges = jnp.where((lane >= 8 * f) & (lane < 8 * f + width), first, edges)
+            edges = jnp.where((lane >= 64 + 8 * f) & (lane < 64 + 8 * f + width), last, edges)
         square[0:ROWS] = edges
         square[ROWS:128] = jnp.zeros((128 - ROWS, 128), F32)
         square[...] = square[...].T
         gxl[...] = square[0:40]
         gxr[...] = square[64:104]
+        for load in load_tabs:
+            load.wait()
+
+
+def table_rows(tabs, i):
+    return jnp.concatenate([jnp.broadcast_to(tabs[i], (8, NW))] * (128 // NW), axis=1)
+
+
+def ratio_kernel(tabs, terrain, ew, sw, up_cols, pool_cols, up_rows, pool_rows, found):
+    group = lax.axis_index("comp")
+
+    @pl.when(group == 1)
+    def _():
+        def columns(shape, fine_axis):
+            fine = lax.broadcasted_iota(jnp.int32, shape, fine_axis)
+            coarse = lax.broadcasted_iota(jnp.int32, shape, 1 - fine_axis)
+            first = jnp.where(coarse == 255, WIDE - AGG, jnp.where(coarse <= 128, AGG * coarse, 2 * WIDE))
+            return jnp.where((fine >= first) & (fine < first + AGG), 1.0, 0.0).astype(BF)
+
+        up_cols[...] = columns((256, WIDE), 1)
+        pool_cols[...] = columns((WIDE, 256), 0)
+
+        def fine_rows(shape, axis):
+            at = lax.broadcasted_iota(jnp.int32, shape, axis)
+            at = jnp.where(at >= 96, at - 96, at)
+            strip = lax.shift_right_logical(at, 3)
+            return STRIPS * (at - 8 * strip) + strip
+
+        fine, coarse = fine_rows((192, 64), 0), lax.broadcasted_iota(jnp.int32, (192, 64), 1)
+        lower = lax.broadcasted_iota(jnp.int32, (192, 64), 0) >= 96
+        mine = jnp.where(coarse >= 32, 1, 0) == jnp.where(lower, 1, 0)
+        coarse = lax.rem(coarse, 16)
+        own = (fine >= AGG * coarse) & (fine < AGG * coarse + AGG) & (coarse < 8)
+        below = (fine >= ROWS) & (fine < ROWS + 8) & (coarse == 8)
+        above = (fine >= ROWS + 8) & (coarse == 15)
+        up_rows[...] = jnp.where(mine & (own | below | above), 1.0, 0.0).astype(BF)
+        fine, coarse = fine_rows((8, 192), 1), lax.broadcasted_iota(jnp.int32, (8, 192), 0)
+        pool_rows[...] = jnp.where((fine >= AGG * coarse) & (fine < AGG * coarse + AGG), 1.0, 0.0).astype(BF)
+
+        for i in range(2):
+            table = table_rows(tabs, 1 + i)
+            for r in range(0, ROWS, 8):
+                for t in range(10):
+                    found[i * ROWS + r : i * ROWS + r + 8, cut(t)] = jnp.take_along_axis(
+                        table, terrain[r : r + 8, cut(t)], axis=1
+                    )
+        part = dot(both(found[...]), pool_cols[0:COLS, 0:128])
+        part = part[0:160] + part[160:320]
+        part = jnp.concatenate([part[0:ROWS], part[ROWS:160]], axis=1)
+        total = dot(twice(within((8, ROWS), 1)), both(part))
+        scale = inverse(total)
+        scale = jnp.concatenate([both(scale[:, 0:128]), both(scale[:, 128:256])], axis=0)
+        wide = dot(scale, up_cols[0:128, 0:COLS]).astype(BF)
+        repeat = twice(within((ROWS, 8), 0))
+        ew[...] = found[0:ROWS] * dot(repeat, wide[0:16])
+        sw[...] = found[ROWS:160] * dot(repeat, wide[16:32])
 
 
 def edges_of_grid():
@@ -277,9 +319,9 @@
 
 
 def prepare_kernel(
-    keff, head, code, ew, sw, from_left, from_right, from_up, from_down, rows_up, rows_down, after,
+    keff, head, code, ew, sw, tabs, up_cols, pool_cols, from_left, from_right, from_up, from_down, rows_up, rows_down, after,
     a_e, a_w, a_n, a_s, a_c, m_e, m_w, m_n, m_s, m_c, head_out, ew_out, sw_out,
-    square, side, nat, kring, cring,
+    square, side, nat, kring, cring, outer, found, near,
 ):
     group = lax.axis_index("comp")
     has_up, has_down, has_left, has_right = edges_of_grid()
@@ -289,25 +331,21 @@
         lane128 = lax.broadcasted_iota(jnp.int32, (40, 128), 1)
 
         def column(own, down, up):
-            down, up = pltpu.roll(down, 80, 1), pltpu.roll(up, 16, 1)
-            return jnp.where(lane128 < 80, own, jnp.where(lane128 < 88, down * has_down, up * has_up))
+            down, up = pltpu.roll(down, 80, 1), pltpu.roll(up, 24, 1)
+            return jnp.where(lane128 < 80, own, jnp.where(lane128 < 92, down * has_down, up * has_up))
 
         square[...] = jnp.zeros((128, 128), F32)
         square[0:40] = column(from_right[...], from_down[40:80], from_up[40:80]) * has_right
         square[64:104] = column(from_left[...], from_down[0:40], from_up[0:40]) * has_left
         side[...] = square[...].T
-        own = (keff, head, code, ew, sw)
-        lane = lax.broadcasted_iota(jnp.int32, (96, 128), 1)
-        for f in range(FIELDS):
-            for t in range(10):
-                at = f * 80 + t * 8
-                nat[t, 0:ROWS] = own[f][:, cut(t)]
-                nat[t, ROWS : ROWS + 8] = rows_down[at : at + 8] * has_down
-                nat[t, ROWS + 8 : ROWS + 16] = rows_up[at : at + 8] * has_up
-            columns = side[0:96]
-            right = columns if f == 0 else pltpu.roll(columns, (-8 * f) % 128, 1)
-            left = pltpu.roll(columns, 120 - 64 - 8 * f, 1)
-            nat[10] = jnp.where(lane < 8, right, jnp.where(lane >= 120, left, 0.0))
+        lane = lax.broadcasted_iota(jnp.int32, (104, 128), 1)
+
+        def columns_of(f, width):
+            right = side[0:104] if f == 0 else pltpu.roll(side[0:104], (-8 * f) % 128, 1)
+            left = pltpu.roll(side[0:104], (64 - 8 * f - width) % 128, 1)
+            return jnp.where(lane < width, right, jnp.where(lane >= 128 - width, left, 0.0))
+
+        def interleave(f):
             for k in range(STRIPS):
                 for t in range(TILES):
                     value = nat[t, pl.ds(k, 8, stride=STRIPS), :]
@@ -323,6 +361,70 @@
                         ew_out[k, :, cut(t)] = jnp.where(active, value, 0.0)
                     else:
                         sw_out[k, :, cut(t)] = value
+
+        for f, own in enumerate((keff, head, code)):
+            for t in range(10):
+                at = f * 80 + t * 8
+                nat[t, 0:ROWS] = own[:, cut(t)]
+                nat[t, ROWS : ROWS + 8] = rows_down[at : at + 8] * has_down
+                nat[t, ROWS + 8 : ROWS + 16] = rows_up[at : at + 8] * has_up
+            columns = columns_of(f, 8)
+            nat[10, 0 : ROWS + 8] = columns[0 : ROWS + 8]
+            nat[10, ROWS + 8 : ROWS + 16] = columns[96:104]
+            interleave(f)
+
+        corner = columns_of(3, AGG)
+        outer[...] = jnp.zeros((32, WIDE), F32)
+        for at, rows in ((0, rows_down), (16, rows_up)):
+            for t in range(10):
+                outer[at : at + 8, cut(t)] = rows[240 + t * 8 : 248 + t * 8]
+                outer[at + 8 : at + 10, cut(t)] = rows[320 + t * 2 : 322 + t * 2]
+        outer[0:10, cut(10)] = corner[80:90]
+        outer[16:24, cut(10)] = corner[96:104]
+        outer[24:26, cut(10)] = corner[94:96]
+        square[0:ROWS] = corner[0:ROWS]
+        for i in range(2):
+            table = table_rows(tabs, 1 + i)
+            for r in range(0, 32, 8):
+                for t in range(TILES):
+                    found[i * 32 + r : i * 32 + r + 8, cut(t)] = jnp.take_along_axis(
+                        table, outer[r : r + 8, cut(t)].astype(jnp.int32), axis=1
+                    )
+            for r in range(0, ROWS, 8):
+                near[i * ROWS + r : i * ROWS + r + 8] = jnp.take_along_axis(
+                    table, square[r : r + 8].astype(jnp.int32), axis=1
+                )
+        part = dot(both(found[...]), pool_cols[...])
+        part = part[0:64] + part[64:128]
+        totals = []
+        for at in (0, 16, 32, 48):
+            totals.append(jnp.sum(part[at : at + 8], axis=0, keepdims=True) + part[at + 8 : at + 9] + part[at + 9 : at + 10])
+        scale = inverse(jnp.concatenate(totals + [jnp.zeros((4, 256), F32)], axis=0))
+        wide = dot(both(scale), up_cols[...])
+        wide = wide[0:8] + wide[8:16]
+
+        col = lax.broadcasted_iota(jnp.int32, (128, 128), 1)
+        row = lax.broadcasted_iota(jnp.int32, (128, 128), 0)
+        ends = jnp.where(((col == 0) & (row < AGG)) | ((col == 1) & (row >= 128 - AGG)), 1.0, 0.0).astype(BF)
+        part = dot(both(near[...]), ends)
+        part = part[0:160] + part[160:320]
+        part = jnp.concatenate([part[0:ROWS], part[ROWS:160]], axis=1)
+        scale = inverse(dot(twice(within((8, ROWS), 1)), both(part)))
+        scale = dot(twice(within((ROWS, 8), 0)), both(scale))
+        first = lax.broadcasted_iota(jnp.int32, (ROWS, 128), 1) < AGG
+        for i, own in enumerate((ew, sw)):
+            for t in range(TILES):
+                nat[t, ROWS : ROWS + 8] = found[32 * i : 32 * i + 8, cut(t)] * wide[2 * i : 2 * i + 1, cut(t)]
+                nat[t, ROWS + 8 : ROWS + 16] = (
+                    found[32 * i + 16 : 32 * i + 24, cut(t)] * wide[2 * i + 1 : 2 * i + 2, cut(t)]
+                )
+            at = 128 * i
+            nat[10, 0:ROWS] = near[i * ROWS : (i + 1) * ROWS] * jnp.where(
+                first, scale[:, at : at + 1], scale[:, at + 1 : at + 2]
+            )
+            for t in range(10):
+                nat[t, 0:ROWS] = own[:, cut(t)]
+            interleave(3 + i)
         for ring in (kring, cring):
             for t in range(TILES):
                 ring[0, :, cut(t)] = pltpu.roll(ring[STRIPS, :, cut(t)], 1, 0)
@@ -367,9 +469,8 @@
     @pl.when(group == 1)
     def _():
         pieces = jnp.concatenate([*split(coarse[0]), *split(coarse[1])], axis=0)
-        wide = dot(pieces, up_cols[...]).astype(BF)
-        excess = dot(up_rows[...], wide[0:32])
-        moist = dot(up_rows[...], wide[32:64])
+        fields = dot(up_rows[...], dot(pieces, up_cols[...]).astype(BF))
+        excess, moist = fields[0:96], fields[96:192]
         pond_a[1 : STRIPS + 1] = head[...] + ew[...] * excess.reshape(STRIPS, 8, WIDE)
         store_a[1 : STRIPS + 1] = sw[...] * moist.reshape(STRIPS, 8, WIDE)
 
@@ -421,10 +522,14 @@
             return carry
 
         lax.fori_loop(0, NSUB // 2, two, 0)
-        for ring, out in ((pond_a, ponded_out), (store_a, stored_out)):
-            high, low = split(ring[1 : STRIPS + 1].reshape(STRIPS * 8, WIDE))
-            part = dot(high, pool_cols[...]) + dot(low, pool_cols[...])
-            out[...] = dot(pool_rows[...], jnp.concatenate([*split(part)], axis=0)) * (1.0 / (AGG * AGG))
+        pieces = []
+        for ring in (pond_a, store_a):
+            pieces.extend(split(ring[1 : STRIPS + 1].reshape(STRIPS * 8, WIDE)))
+        part = dot(jnp.concatenate(pieces, axis=0), pool_cols[:, 0:128])
+        part = jnp.concatenate([part[0:96] + part[96:192], part[192:288] + part[288:384]], axis=1)
+        mean = dot(pool_rows[...], both(part)) * (1.0 / (AGG * AGG))
+        ponded_out[...] = mean[:, 0:128]
+        stored_out[...] = mean[:, 128:256]
 
 
 def moved(array, mesh_shape, target):
@@ -456,7 +561,6 @@
 ):
     shape = tuple(lax.axis_size(axis) for axis in ("comp", "gy", "gx"))
     group = lax.axis_index("comp")
-    m = tables()
     params = pltpu.CompilerParams(vmem_limit_bytes=32 * 1024 * 1024)
     arguments = (
         column_water[0].reshape(128, 128), land_soil[0], level_weight[None], excess_weight[None], soil_weight[None],
@@ -465,18 +569,17 @@
     hbm = pl.BlockSpec(memory_space=pltpu.HBM)
     fine = f32(ROWS, COLS)
     fine_int = pltpu.VMEM((ROWS, COLS), jnp.int32)
-    gxl, gxr, main_up, main_down, gyu, gyd, water, soil, weight, keff, head, code, ew, sw = pl.pallas_call(
+    gxl, gxr, main_up, main_down, gyu, gyd, water, soil, weight, tabs, terrain, keff, head, code = pl.pallas_call(
         pack_kernel,
         in_specs=[hbm] * 10,
         out_shape=[f32(40, 128)] * 2
         + [f32(56, 128)] * 2
-        + [f32(400, 128)] * 2
-        + [f32(128, 128), f32(8, 128), f32(LEV, 128)]
-        + [fine] * 5,
+        + [f32(344, 128)] * 2
+        + [f32(128, 128), f32(8, 128), f32(LEV, 128), f32(3, 1, NW)]
+        + [jax.ShapeDtypeStruct((ROWS, COLS), jnp.int32)]
+        + [fine] * 3,
         scratch_shapes=[
             pltpu.VMEM((128, 128), F32),
-            pltpu.VMEM((3, 1, NW), F32),
-            fine_int,
             fine_int,
             fine_int,
             pltpu.SemaphoreType.DMA((2 + 5 * CHUNKS,)),
@@ -484,6 +587,14 @@
         compiler_params=params,
         name="pack",
     )(*(pltpu.with_memory_space_constraint(array, pltpu.HBM) for array in arguments))
+    ew, sw, up_cols, pool_cols, up_rows, pool_rows = pl.pallas_call(
+        ratio_kernel,
+        out_shape=[fine] * 2
+        + [jax.ShapeDtypeStruct(dims, BF) for dims in ((256, WIDE), (WIDE, 256), (192, 64), (8, 192))],
+        scratch_shapes=[pltpu.VMEM((2 * ROWS, COLS), F32)],
+        compiler_params=params,
+        name="ratio",
+    )(tabs, terrain)
     from_left = moved(gxr, shape, lambda g, y, x: (g, y, x + 1))
     from_right = moved(gxl, shape, lambda g, y, x: (g, y, x - 1))
     rows_up = moved(gyd, shape, lambda g, y, x: (g, y + 1, x) if g else (g, y, x ^ 1))
@@ -513,10 +624,16 @@
             pltpu.VMEM((TILES, 96, 128), F32),
             ring,
             ring,
+            pltpu.VMEM((32, WIDE), F32),
+            pltpu.VMEM((64, WIDE), F32),
+            pltpu.VMEM((2 * ROWS, 128), F32),
         ],
         compiler_params=params,
         name="prepare",
-    )(keff, head, code, ew, sw, from_left, from_right, route_up, route_down, rows_up, rows_down, water_top)
+    )(
+        keff, head, code, ew, sw, tabs, up_cols, pool_cols, from_left, from_right, route_up, route_down,
+        rows_up, rows_down, water_top,
+    )
     ring = pltpu.VMEM((STRIPS + 2, 8, WIDE), F32)
     ponded, stored = pl.pallas_call(
         route_kernel,
@@ -524,7 +641,7 @@
         scratch_shapes=[ring] * 4,
         compiler_params=params,
         name="route",
-    )(arrived, *prepared, m["up_cols"], m["up_rows"], m["pool_cols"], m["pool_rows"])
+    )(arrived, *prepared, up_cols, up_rows, pool_cols, pool_rows)
     returned = moved(stored, shape, lambda g, y, x: (1 - g, y, x))
     land_out = returned / (1.0 + evaporation_scale * water_top * water_top)
     return jnp.where(group == 0, land_out, ponded)[None]

time: 37.9 us -> 34.8 us (0.918)
  starting transfers between devices: 24.7 us -> 22.1 us
  waiting for transfers between devices: 10.7 us -> 10.3 us
    ppermute x10, starting transfers between devices: 24.7 us -> 22.1 us  [moved(): return lax.ppermute(array, ('comp', 'gy', 'gx'), pairs)]
    ppermute x10, waiting for transfers between devices: 10.7 us -> 10.3 us  [moved(): return lax.ppermute(array, ('comp', 'gy', 'gx'), pairs)]
where the time goes in v2:
time: 34.8 us; the launch traced here: 34.7 us
  starting transfers between devices  22.1 us (64%)
  waiting for transfers between devices  10.3 us (30%)
  Pallas kernels  1.51 us (4%)
  other arithmetic  0.62 us (2%)
    ppermute x10, starting transfers between devices, moved(): return lax.ppermute(array, ('comp', 'gy', 'gx'), pairs)  22.1 us
    ppermute x10, waiting for transfers between devices, moved(): return lax.ppermute(array, ('comp', 'gy', 'gx'), pairs)  10.3 us
    pallas_call x1, Pallas kernels, per_device(): pl.pallas_call(pack_kernel, in_specs=[hbm] * 10, out_shape=[f32(40, 128)]...  1.06 us
  transfers between devices with their start and end apart: 10, of which 6 were waited for; matrix products, arithmetic and copies ran while one was open for 0% of the time, Pallas kernels for 1%

profile of v2, /device:TPU:0, one launch (start us, length us, event | category | flops | bytes accessed | tf_op | source)
XLA Modules:
  0.0 34.7 jit_solution(10763492265749024018)
XLA Ops:
  0.0 1.1 %pack.1 = (f32[40,128]{1,0:T(8,128)S(1)}, f32[40,128]{1,0:T(8,128)S(1)}, f32[56,128]{1,0:T(8,128)S(1)}, f32[56,128]{1,0:T(8,128)S(1)}, f32[344,128]{1,0:T(8,128)...) custom-call(f32[128,128]{1,0:T(8,128)} %bitcast.15, ...), custom_call_target="tpu_custom_call" | custom-call | tf_op jit(solution)/shard_map/pack/pallas_call | solution.py:572
  1.1 2.5 %collective-permute-start.1 = (f32[40,128]{1,0:T(8,128)S(1)}, f32[40,128]{1,0:T(8,128)S(1)}, u32[]{:S(2)}, u32[]{:S(2)}) collective-permute-start(f32[40,128]{1,0:T(8,128)S(1)} %get-tuple-element.46), channel_id=1, source_target_pairs={{0,7},{1,0},{2,1},{3,2},{4,3},{5,4},{6,5},{7,6},{8,15},{9,8},{10,9... | collective-permute-start | bytes 61448 | tf_op jit(solution)/shard_map/ppermute | solution.py:543
  3.6 0.0 collective-permute-start
  3.6 0.0 collective-permute-start.7
  3.6 0.5 %collective-permute-start.8 = (f32[344,128]{1,0:T(8,128)S(1)}, f32[344,128]{1,0:T(8,128)S(1)}, u32[]{:S(2)}, u32[]{:S(2)}) collective-permute-start(f32[344,128]{1,0:T(8,128)S(1)} %get-tuple-element.60), channel_id=1, source_target_pairs={{0,1},{1,0},{2,3},{3,2},{4,5},{5,4},{6,7},{7,6},{8,9},{9,8},{10,11... | collective-permute-start | bytes 528392 | tf_op jit(solution)/shard_map/ppermute | solution.py:543
  4.1 1.0 %collective-permute-done.1.from_right = f32[40,128]{1,0:T(8,128)S(1)} collective-permute-done((f32[40,128]{1,0:T(8,128)S(1)}, f32[40,128]{1,0:T(8,128)S(1)}, u32[]{:S(2)}, u32[]{:S(2)}) %collective-permute-start.1) | collective-permute-done | bytes 20512 | tf_op jit(solution)/shard_map/ppermute | solution.py:543
  5.1 2.9 %collective-permute-done.from_left = f32[40,128]{1,0:T(8,128)S(1)} collective-permute-done((f32[40,128]{1,0:T(8,128)S(1)}, f32[40,128]{1,0:T(8,128)S(1)}, u32[]{:S(2)}, u32[]{:S(2)}) %collective-permute-start) | collective-permute-done | bytes 20512 | tf_op jit(solution)/shard_map/ppermute | solution.py:543
  8.0 2.0 %collective-permute-start.2 = (f32[88,128]{1,0:T(8,128)S(1)}, f32[88,128]{1,0:T(8,128)S(1)}, u32[]{:S(2)}, u32[]{:S(2)}) collective-permute-start(f32[88,128]{1,0:T(8,128)S(1)} %get-tuple-element.80), channel_id=1, source_target_pairs={{0,8},{1,9},{2,10},{3,11},{4,12},{5,13},{6,14},{7,15},{8,16},{9,17... | collective-permute-start | bytes 135176 | tf_op jit(solution)/shard_map/ppermute | solution.py:543
  10.0 2.3 %collective-permute-start.3 = (f32[88,128]{1,0:T(8,128)S(1)}, f32[88,128]{1,0:T(8,128)S(1)}, u32[]{:S(2)}, u32[]{:S(2)}) collective-permute-start(f32[88,128]{1,0:T(8,128)S(1)} %get-tuple-element.79), channel_id=1, source_target_pairs={{0,56},{1,57},{2,58},{3,59},{4,60},{5,61},{6,62},{7,63},{8,0},{9,1... | collective-permute-start | bytes 135176 | tf_op jit(solution)/shard_map/ppermute | solution.py:543
  12.3 0.0 collective-permute-start.5
  12.3 2.1 %collective-permute-done.2.from_up = f32[88,128]{1,0:T(8,128)S(1)} collective-permute-done((f32[88,128]{1,0:T(8,128)S(1)}, f32[88,128]{1,0:T(8,128)S(1)}, u32[]{:S(2)}, u32[]{:S(2)}) %collective-permute-start.2) | collective-permute-done | bytes 45088 | tf_op jit(solution)/shard_map/ppermute | solution.py:543
  14.4 0.0 collective-permute-start.6
  14.4 0.2 collective-permute-done.3.from_down
  14.6 0.4 %land.1 = (f32[2,16,256]{2,1,0:T(8,128)S(1)}, f32[8,128]{1,0:T(8,128)S(1)}) custom-call(f32[128,128]{1,0:T(8,128)S(1)} %get-tuple-element.42.water, f32[8,128]{1,0:T(8,128)S(1)} %get-tuple-element.43.soil, f32[16,128]{1,0:T(8,128)S(1)} %get-tuple-element.44.weight, f32[40,128]{1,0:T(8,128)S(1)} %collective-permute-done.from_left, ...), custom_call_target="tpu_custom_call" | custom-call | tf_op jit(solution)/shard_map/land/pallas_call | solution.py:608
  15.0 2.8 %collective-permute-start.4 = (f32[2,16,256]{2,1,0:T(8,128)S(1)}, f32[2,16,256]{2,1,0:T(8,128)S(1)}, u32[]{:S(2)}, u32[]{:S(2)}) collective-permute-start(f32[2,16,256]{2,1,0:T(8,128)S(1)} %get-tuple-element.49), channel_id=1, source_target_pairs={{0,64},{1,65},{2,66},{3,67},{4,68},{5,69},{6,70},{7,71},{8,72},{9,... | collective-permute-start | bytes 98312 | tf_op jit(solution)/shard_map/ppermute | solution.py:543
  17.8 0.0 collective-permute-done.5.from_up
  17.8 0.0 collective-permute-done.6.from_down
  17.8 0.0 collective-permute-done.7.rows_up
  17.8 0.0 collective-permute-done.8.rows_down
  17.9 2.6 %collective-permute-done.4.coarse = f32[2,16,256]{2,1,0:T(8,128)S(1)} collective-permute-done((f32[2,16,256]{2,1,0:T(8,128)S(1)}, f32[2,16,256]{2,1,0:T(8,128)S(1)}, u32[]{:S(2)}, u32[]{:S(2)}) %collective-permute-start.4) | collective-permute-done | bytes 32800 | tf_op jit(solution)/shard_map/ppermute | solution.py:543
  20.5 12.0 %collective-permute-start.9 = (f32[8,128]{1,0:T(8,128)S(1)}, f32[8,128]{1,0:T(8,128)S(1)}, u32[]{:S(2)}, u32[]{:S(2)}) collective-permute-start(f32[8,128]{1,0:T(8,128)S(1)} %get-tuple-element.77), channel_id=1, source_target_pairs={{0,64},{1,65},{2,66},{3,67},{4,68},{5,69},{6,70},{7,71},{8,72},{9,... | collective-permute-start | bytes 12296 | tf_op jit(solution)/shard_map/ppermute | solution.py:543
  32.5 1.6 %collective-permute-done.9 = f32[8,128]{1,0:T(8,128)S(1)} collective-permute-done((f32[8,128]{1,0:T(8,128)S(1)}, f32[8,128]{1,0:T(8,128)S(1)}, u32[]{:S(2)}, u32[]{:S(2)}) %collective-permute-start.9) | collective-permute-done | bytes 4128 | tf_op jit(solution)/shard_map/ppermute | solution.py:543
  34.1 0.6 %fusion.4 = f32[1,8,128]{2,1,0:T(8,128)} fusion(f32[8,128]{1,0:T(8,128)S(1)} %get-tuple-element.78, f32[8,128]{1,0:T(8,128)S(1)} %collective-permute-done.9, f32[8,128]{1,0:T(8,128)S(1)} %get-tuple-element.61.after, pred[]{:T(512)S(6)} %eq.3), kind=kLoop, calls=%fused_computation.9 | loop fusion | flops 5120 | bytes 16385 | tf_op jit(solution)/shard_map/broadcast_in_dim | solution.py:647
  (8 shorter events, 0.1 us)
Async XLA Ops:
  1.1 4.0 %collective-permute-start.1 = (f32[40,128]{1,0:T(8,128)S(1)}, f32[40,128]{1,0:T(8,128)S(1)}, u32[]{:S(2)}, u32[]{:S(2)}) collective-permute-start(f32[40,128]{1,0:T(8,128)S(1)} %get-tuple-element.46), channel_id=1, source_target_pairs={{0,7},{1,0},{2,1},{3,2},{4,3},{5,4},{6,5},{7,6},{8,15},{9,8},{10,9... | collective-permute-start | bytes 61448 | tf_op jit(solution)/shard_map/ppermute | solution.py:543
  3.6 4.4 %collective-permute-start = (f32[40,128]{1,0:T(8,128)S(1)}, f32[40,128]{1,0:T(8,128)S(1)}, u32[]{:S(2)}, u32[]{:S(2)}) collective-permute-start(f32[40,128]{1,0:T(8,128)S(1)} %get-tuple-element.45), channel_id=1, source_target_pairs={{0,1},{1,2},{2,3},{3,4},{4,5},{5,6},{6,7},{7,0},{8,9},{9,10},{10,1... | collective-permute-start | bytes 61448 | tf_op jit(solution)/shard_map/ppermute | solution.py:543
  3.6 14.2 %collective-permute-start.7 = (f32[344,128]{1,0:T(8,128)S(1)}, f32[344,128]{1,0:T(8,128)S(1)}, u32[]{:S(2)}, u32[]{:S(2)}) collective-permute-start(f32[344,128]{1,0:T(8,128)S(1)} %get-tuple-element.59), channel_id=1, source_target_pairs={{0,1},{1,0},{2,3},{3,2},{4,5},{5,4},{6,7},{7,6},{8,9},{9,8},{10,11... | collective-permute-start | bytes 528392 | tf_op jit(solution)/shard_map/ppermute | solution.py:543
  3.6 14.2 %collective-permute-start.8 = (f32[344,128]{1,0:T(8,128)S(1)}, f32[344,128]{1,0:T(8,128)S(1)}, u32[]{:S(2)}, u32[]{:S(2)}) collective-permute-start(f32[344,128]{1,0:T(8,128)S(1)} %get-tuple-element.60), channel_id=1, source_target_pairs={{0,1},{1,0},{2,3},{3,2},{4,5},{5,4},{6,7},{7,6},{8,9},{9,8},{10,11... | collective-permute-start | bytes 528392 | tf_op jit(solution)/shard_map/ppermute | solution.py:543
  8.0 6.3 %collective-permute-start.2 = (f32[88,128]{1,0:T(8,128)S(1)}, f32[88,128]{1,0:T(8,128)S(1)}, u32[]{:S(2)}, u32[]{:S(2)}) collective-permute-start(f32[88,128]{1,0:T(8,128)S(1)} %get-tuple-element.80), channel_id=1, source_target_pairs={{0,8},{1,9},{2,10},{3,11},{4,12},{5,13},{6,14},{7,15},{8,16},{9,17... | collective-permute-start | bytes 135176 | tf_op jit(solution)/shard_map/ppermute | solution.py:543
  10.0 4.5 %collective-permute-start.3 = (f32[88,128]{1,0:T(8,128)S(1)}, f32[88,128]{1,0:T(8,128)S(1)}, u32[]{:S(2)}, u32[]{:S(2)}) collective-permute-start(f32[88,128]{1,0:T(8,128)S(1)} %get-tuple-element.79), channel_id=1, source_target_pairs={{0,56},{1,57},{2,58},{3,59},{4,60},{5,61},{6,62},{7,63},{8,0},{9,1... | collective-permute-start | bytes 135176 | tf_op jit(solution)/shard_map/ppermute | solution.py:543
  12.3 5.5 %collective-permute-start.5 = (f32[80,128]{1,0:T(8,128)S(1)}, f32[80,128]{1,0:T(8,128)S(1)}, u32[]{:S(2)}, u32[]{:S(2)}) collective-permute-start(f32[80,128]{1,0:T(8,128)S(1)} %constant_dynamic-update-slice_fusion), channel_id=1, source_target_pairs={{0,1},{1,0},{2,3},{3,2},{4,5},{5,4},{6,7},{7,6},{8,9},{9,8},{10,11... | collective-permute-start | bytes 122888 | tf_op jit(solution)/shard_map/ppermute | solution.py:543
  14.4 3.5 %collective-permute-start.6 = (f32[80,128]{1,0:T(8,128)S(1)}, f32[80,128]{1,0:T(8,128)S(1)}, u32[]{:S(2)}, u32[]{:S(2)}) collective-permute-start(f32[80,128]{1,0:T(8,128)S(1)} %constant_dynamic-update-slice_fusion), channel_id=1, source_target_pairs={{0,1},{1,0},{2,3},{3,2},{4,5},{5,4},{6,7},{7,6},{8,9},{9,8},{10,11... | collective-permute-start | bytes 122888 | tf_op jit(solution)/shard_map/ppermute | solution.py:543
  15.0 5.5 %collective-permute-start.4 = (f32[2,16,256]{2,1,0:T(8,128)S(1)}, f32[2,16,256]{2,1,0:T(8,128)S(1)}, u32[]{:S(2)}, u32[]{:S(2)}) collective-permute-start(f32[2,16,256]{2,1,0:T(8,128)S(1)} %get-tuple-element.49), channel_id=1, source_target_pairs={{0,64},{1,65},{2,66},{3,67},{4,68},{5,69},{6,70},{7,71},{8,72},{9,... | collective-permute-start | bytes 98312 | tf_op jit(solution)/shard_map/ppermute | solution.py:543
  20.5 13.6 %collective-permute-start.9 = (f32[8,128]{1,0:T(8,128)S(1)}, f32[8,128]{1,0:T(8,128)S(1)}, u32[]{:S(2)}, u32[]{:S(2)}) collective-permute-start(f32[8,128]{1,0:T(8,128)S(1)} %get-tuple-element.77), channel_id=1, source_target_pairs={{0,64},{1,65},{2,66},{3,67},{4,68},{5,69},{6,70},{7,71},{8,72},{9,... | collective-permute-start | bytes 12296 | tf_op jit(solution)/shard_map/ppermute | solution.py:543

commit v3 on v2

--- a/solution.py
+++ b/solution.py
@@ -24,6 +24,7 @@
 drainage_rate = 0.1
 half_point = 0.1
 evaporation_scale = 0.5
+SCALE = 1.0 / infiltration_rate
 
 
 def split(x):
@@ -86,20 +87,20 @@
         ]
         for load in loads:
             load.start()
-        gxl[16:40] = jnp.zeros((24, 128), F32)
-        gxr[16:40] = jnp.zeros((24, 128), F32)
+        gxl[...] = jnp.zeros((40, 128), F32)
+        gxr[...] = jnp.zeros((40, 128), F32)
         square[16:128] = jnp.zeros((112, 128), F32)
         for load in loads:
             load.wait()
         square[0:8] = soil[...]
         square[8:9, 0:LEV] = tabs[0]
         turned = square[...].T
-        gxl[8:16] = turned[0:8]
-        gxr[8:16] = turned[120:128]
+        gxl[3:4] = turned[0:1]
+        gxr[4:5] = turned[127:128]
         weight[...] = jnp.broadcast_to(turned[0:LEV, 8:9], (LEV, 128))
         square[...] = water[...].T
-        gxl[0:8] = square[0:8]
-        gxr[0:8] = square[120:128]
+        gxl[0:3] = square[0:3]
+        gxr[5:8] = square[125:128]
         for j in range(3):
             for h in range(2):
                 at = j * 16 + h * 8
@@ -169,7 +170,7 @@
         square[ROWS:128] = jnp.zeros((128 - ROWS, 128), F32)
         square[...] = square[...].T
         gxl[...] = square[0:40]
-        gxr[...] = square[64:104]
+        gxr[...] = pltpu.roll(square[64:104], 48, 1)
         for load in load_tabs:
             load.wait()
 
@@ -247,8 +248,8 @@
     def _():
         pairs = (
             (from_right[0:8], from_left[0:8]),
-            (from_down[16:24], from_down[0:8]),
-            (from_up[16:24], from_up[0:8]),
+            (from_down[0:8], from_down[0:8]),
+            (from_up[0:8], from_up[0:8]),
         )
         square[8:120] = jnp.zeros((112, 128), F32)
         for i, (right, left) in enumerate(pairs):
@@ -257,8 +258,8 @@
             side[i] = square[...].T
         lane = lanes()
         for at, (own, down, up) in (
-            (0, (from_right[8:16], from_down[24:32], from_up[24:32])),
-            (120, (from_left[8:16], from_down[8:16], from_up[8:16])),
+            (0, [pltpu.roll(x[0:8], 5, 0) for x in (from_right, from_down, from_up)]),
+            (120, [pltpu.roll(x[0:8], 3, 0) for x in (from_left, from_down, from_up)]),
         ):
             square[at : at + 8] = jnp.where(
                 lane < 8, own, jnp.where(lane < 16, pltpu.roll(down, 8, 1), pltpu.roll(up, 16, 1))
@@ -280,12 +281,12 @@
 
         field = []
         for j in range(3):
-            tile = from_up[32 + j * 16 : 48 + j * 16]
+            tile = from_up[8 + j * 16 : 24 + j * 16]
             field.append(jnp.concatenate([tile, side_levels(2, 5 + j)], axis=1) * (col_ok * has_up))
         for j in range(8):
             field.append(jnp.concatenate([levels(water, j), side_levels(0, j)], axis=1) * col_ok)
         for j in range(3):
-            tile = from_down[32 + j * 16 : 48 + j * 16]
+            tile = from_down[8 + j * 16 : 24 + j * 16]
             field.append(jnp.concatenate([tile, side_levels(1, j)], axis=1) * (col_ok * has_down))
 
         def sweep(old, first, last):
@@ -308,14 +309,14 @@
         moist = jnp.concatenate(
             [
                 jnp.concatenate([soil[...], side_soil[0:8]], axis=1),
-                jnp.concatenate([from_down[80:81], side_soil[8:9]], axis=1),
+                jnp.concatenate([from_down[56:57], side_soil[8:9]], axis=1),
                 blank,
-                jnp.concatenate([from_up[87:88], side_soil[23:24]], axis=1),
+                jnp.concatenate([from_up[63:64], side_soil[23:24]], axis=1),
             ],
             axis=0,
         )
-        coarse[0] = rain * moist * moist / (moist * moist + half_point)
-        coarse[1] = moist
+        coarse[0] = SCALE * rain * moist * moist / (moist * moist + half_point)
+        coarse[1] = SCALE * moist
 
 
 def prepare_kernel(
@@ -331,12 +332,14 @@
         lane128 = lax.broadcasted_iota(jnp.int32, (40, 128), 1)
 
         def column(own, down, up):
-            down, up = pltpu.roll(down, 80, 1), pltpu.roll(up, 24, 1)
             return jnp.where(lane128 < 80, own, jnp.where(lane128 < 92, down * has_down, up * has_up))
 
         square[...] = jnp.zeros((128, 128), F32)
-        square[0:40] = column(from_right[...], from_down[40:80], from_up[40:80]) * has_right
-        square[64:104] = column(from_left[...], from_down[0:40], from_up[0:40]) * has_left
+        down, up = from_down[0:40], from_up[0:40]
+        square[0:40] = has_right * column(from_right[...], pltpu.roll(down, 80, 1), pltpu.roll(up, 24, 1))
+        square[64:104] = has_left * column(
+            pltpu.roll(from_left[...], 80, 1), pltpu.roll(down, 32, 1), pltpu.roll(up, 104, 1)
+        )
         side[...] = square[...].T
         lane = lax.broadcasted_iota(jnp.int32, (104, 128), 1)
 
@@ -353,7 +356,7 @@
                         kring[k + 1, :, cut(t)] = value
                     elif f == 1:
                         active = kring[k + 1, :, cut(t)] > 0.0
-                        head_out[k, :, cut(t)] = jnp.where(active, value, 0.0)
+                        head_out[k, :, cut(t)] = jnp.where(active, SCALE * value, 0.0)
                     elif f == 2:
                         cring[k + 1, :, cut(t)] = value
                     elif f == 3:
@@ -430,14 +433,14 @@
                 ring[0, :, cut(t)] = pltpu.roll(ring[STRIPS, :, cut(t)], 1, 0)
                 ring[STRIPS + 1, :, cut(t)] = pltpu.roll(ring[1, :, cut(t)], 7, 0)
 
-        def strip(k, carry):
-            lane = lanes()
+        lane = lanes()
+        for k in range(STRIPS):
             here = [kring[k + 1, :, cut(t)] for t in range(TILES)]
             codes = [cring[k + 1, :, cut(t)] for t in range(TILES)]
             west, east = beside(here, lane)
 
             def drains(cond, codes, number):
-                return jnp.where((cond > 0.0) & (codes == number), drainage_rate, 0.0)
+                return jnp.where((cond > 0.0) & (codes == number), drainage_rate / SCALE, 0.0)
 
             to_east, _ = beside([drains(here[t], codes[t], 3.0) for t in range(TILES)], lane)
             _, to_west = beside([drains(here[t], codes[t], 2.0) for t in range(TILES)], lane)
@@ -454,15 +457,12 @@
                 m_s[k, :, cut(t)] = drains(south, cring[k + 2, :, cut(t)], 0.0)
                 m_w[k, :, cut(t)] = to_east[t]
                 m_e[k, :, cut(t)] = to_west[t]
-                m_c[k, :, cut(t)] = jnp.where(here[t] > 0.0, drainage_rate, 0.0)
-            return carry
-
-        lax.fori_loop(0, STRIPS, strip, 0)
+                m_c[k, :, cut(t)] = jnp.where(here[t] > 0.0, drainage_rate / SCALE, 0.0)
 
 
 def route_kernel(
     coarse, a_e, a_w, a_n, a_s, a_c, m_e, m_w, m_n, m_s, m_c, head, ew, sw, up_cols, up_rows, pool_cols, pool_rows,
-    ponded_out, stored_out, pond_a, pond_b, store_a, store_b,
+    ponded_out, stored_out, pond_a, pond_b, store, square_a, square_b,
 ):
     group = lax.axis_index("comp")
 
@@ -472,7 +472,8 @@
         fields = dot(up_rows[...], dot(pieces, up_cols[...]).astype(BF))
         excess, moist = fields[0:96], fields[96:192]
         pond_a[1 : STRIPS + 1] = head[...] + ew[...] * excess.reshape(STRIPS, 8, WIDE)
-        store_a[1 : STRIPS + 1] = sw[...] * moist.reshape(STRIPS, 8, WIDE)
+        store[...] = sw[...] * moist.reshape(STRIPS, 8, WIDE)
+        square_a[1 : STRIPS + 1] = store[...] * store[...]
 
         def close(ring):
             for t in range(TILES):
@@ -480,54 +481,50 @@
                 ring[STRIPS + 1, :, cut(t)] = pltpu.roll(ring[1, :, cut(t)], 7, 0)
 
         close(pond_a)
-        close(store_a)
-
-        def substep(pond, store, new_pond, new_store):
+        close(square_a)
+
+        def substep(pond, square, new_pond, new_square):
             lane = lanes()
             first, last = lane == 0, lane == 127
             for k in range(STRIPS):
-                p, s = pond[k + 1, :, cut(0)], store[k + 1, :, cut(0)]
-                q = s * s
+                p, q = pond[k + 1, :, cut(0)], square[k + 1, :, cut(0)]
                 p_left, q_left = pltpu.roll(p, 127, 1), pltpu.roll(q, 127, 1)
-                s_r = store[k + 1, :, cut(TILES - 1)]
                 p_before = pltpu.roll(pond[k + 1, :, cut(TILES - 1)], 1, 1)
-                q_before = pltpu.roll(s_r * s_r, 1, 1)
+                q_before = pltpu.roll(square[k + 1, :, cut(TILES - 1)], 1, 1)
                 for t in range(TILES):
                     c, after = cut(t), cut((t + 1) % TILES)
-                    p_next, s_next = pond[k + 1, :, after], store[k + 1, :, after]
-                    q_next = s_next * s_next
+                    p_next, q_next = pond[k + 1, :, after], square[k + 1, :, after]
                     p_right, q_right = pltpu.roll(p, 1, 1), pltpu.roll(q, 1, 1)
                     p_next_left, q_next_left = pltpu.roll(p_next, 127, 1), pltpu.roll(q_next, 127, 1)
                     p_w, p_e = jnp.where(first, p_before, p_right), jnp.where(last, p_next_left, p_left)
                     q_w, q_e = jnp.where(first, q_before, q_right), jnp.where(last, q_next_left, q_left)
-                    s_n, s_s = store[k, :, c], store[k + 2, :, c]
-                    below = 1.0 + s
-                    guess = pltpu.reciprocal(below, approx=True)
-                    guess = guess * (2.0 - below * guess)
-                    soaked = infiltration_rate * p * guess
+                    s = store[k, :, c]
+                    soaked = p * pltpu.reciprocal(SCALE + s, approx=True)
                     flow = a_n[k, :, c] * pond[k, :, c] + a_s[k, :, c] * pond[k + 2, :, c]
                     flow = flow + (a_w[k, :, c] * p_w + a_e[k, :, c] * p_e)
                     new_pond[k + 1, :, c] = a_c[k, :, c] * p + flow - soaked
-                    inflow = m_n[k, :, c] * (s_n * s_n) + m_s[k, :, c] * (s_s * s_s)
+                    inflow = m_n[k, :, c] * square[k, :, c] + m_s[k, :, c] * square[k + 2, :, c]
                     inflow = inflow + (m_w[k, :, c] * q_w + m_e[k, :, c] * q_e)
-                    new_store[k + 1, :, c] = s + soaked - m_c[k, :, c] * q + inflow
-                    p, s, q, p_left, q_left = p_next, s_next, q_next, p_next_left, q_next_left
+                    s = (s + soaked) + (inflow - m_c[k, :, c] * q)
+                    store[k, :, c] = s
+                    new_square[k + 1, :, c] = s * s
+                    p, q, p_left, q_left = p_next, q_next, p_next_left, q_next_left
                     p_before, q_before = p_right, q_right
             close(new_pond)
-            close(new_store)
+            close(new_square)
 
         def two(i, carry):
-            substep(pond_a, store_a, pond_b, store_b)
-            substep(pond_b, store_b, pond_a, store_a)
+            substep(pond_a, square_a, pond_b, square_b)
+            substep(pond_b, square_b, pond_a, square_a)
             return carry
 
         lax.fori_loop(0, NSUB // 2, two, 0)
         pieces = []
-        for ring in (pond_a, store_a):
-            pieces.extend(split(ring[1 : STRIPS + 1].reshape(STRIPS * 8, WIDE)))
+        for last in (pond_a[1 : STRIPS + 1], store[...]):
+            pieces.extend(split(last.reshape(STRIPS * 8, WIDE)))
         part = dot(jnp.concatenate(pieces, axis=0), pool_cols[:, 0:128])
         part = jnp.concatenate([part[0:96] + part[96:192], part[192:288] + part[288:384]], axis=1)
-        mean = dot(pool_rows[...], both(part)) * (1.0 / (AGG * AGG))
+        mean = dot(pool_rows[...], both(part)) * (1.0 / (SCALE * AGG * AGG))
         ponded_out[...] = mean[:, 0:128]
         stored_out[...] = mean[:, 128:256]
 
@@ -599,12 +596,21 @@
     from_right = moved(gxl, shape, lambda g, y, x: (g, y, x - 1))
     rows_up = moved(gyd, shape, lambda g, y, x: (g, y + 1, x) if g else (g, y, x ^ 1))
     rows_down = moved(gyu, shape, lambda g, y, x: (g, y - 1, x) if g else (g, y, x ^ 1))
-    land = [from_left[:16], from_right[:16]]
-    land_up = moved(jnp.concatenate(land + [main_down]), shape, lambda g, y, x: (g, y, x ^ 1) if g else (g, y + 1, x))
-    land_down = moved(jnp.concatenate(land + [main_up]), shape, lambda g, y, x: (g, y, x ^ 1) if g else (g, y - 1, x))
-    route = jnp.concatenate([from_left, from_right])
-    route_up = moved(route, shape, lambda g, y, x: (g, y + 1, x) if g else (g, y, x ^ 1))
-    route_down = moved(route, shape, lambda g, y, x: (g, y - 1, x) if g else (g, y, x ^ 1))
+    row = lax.broadcasted_iota(jnp.int32, (8, 128), 0)
+    halo = jnp.where(row < 4, from_right[:8], from_left[:8])
+    land_up = moved(
+        jnp.concatenate([halo, main_down]), shape, lambda g, y, x: (g, y, x ^ 1) if g else (g, y + 1, x)
+    )
+    land_down = moved(
+        jnp.concatenate([halo, main_up]), shape, lambda g, y, x: (g, y, x ^ 1) if g else (g, y - 1, x)
+    )
+    lane = lax.broadcasted_iota(jnp.int32, (40, 128), 1)
+    route_up = moved(
+        jnp.concatenate([jnp.where(lane < 100, from_right, from_left), jnp.zeros((32, 128), F32)]), shape, lambda g, y, x: (g, y + 1, x) if g else (g, y, x ^ 1)
+    )
+    route_down = moved(
+        jnp.concatenate([jnp.where(lane < 40, from_right, from_left), jnp.zeros((32, 128), F32)]), shape, lambda g, y, x: (g, y - 1, x) if g else (g, y, x ^ 1)
+    )
     coarse, water_top = pl.pallas_call(
         land_kernel,
         out_shape=[f32(2, 16, 256), f32(8, 128)],
@@ -638,7 +644,7 @@
     ponded, stored = pl.pallas_call(
         route_kernel,
         out_shape=[f32(8, 128), f32(8, 128)],
-        scratch_shapes=[ring] * 4,
+        scratch_shapes=[ring] * 2 + [pltpu.VMEM((STRIPS, 8, WIDE), F32)] + [ring] * 2,
         compiler_params=params,
         name="route",
     )(arrived, *prepared, up_cols, up_rows, pool_cols, pool_rows)

time: 34.8 us -> 32.5 us (0.934)
  waiting for transfers between devices: 10.3 us -> 6.38 us
  starting transfers between devices: 22.1 us -> 23.7 us
    ppermute x10, waiting for transfers between devices: 10.3 us -> 6.38 us  [moved(): return lax.ppermute(array, ('comp', 'gy', 'gx'), pairs)]
    ppermute x10, starting transfers between devices: 22.1 us -> 23.7 us  [moved(): return lax.ppermute(array, ('comp', 'gy', 'gx'), pairs)]
  transfers between devices with their start and end apart: 10 -> 10, of which waited for: 6 -> 5; matrix products, arithmetic and copies ran while one was open for 0% -> 0% of each run, Pallas kernels for 1% -> 1%
where the time goes in v3:
time: 32.5 us; the launch traced here: 32.3 us
  starting transfers between devices  23.7 us (73%)
  waiting for transfers between devices  6.38 us (20%)
  Pallas kernels  1.52 us (5%)
  other arithmetic  0.7 us (2%)
    ppermute x10, starting transfers between devices, moved(): return lax.ppermute(array, ('comp', 'gy', 'gx'), pairs)  23.7 us
    ppermute x10, waiting for transfers between devices, moved(): return lax.ppermute(array, ('comp', 'gy', 'gx'), pairs)  6.38 us
    pallas_call x1, Pallas kernels, per_device(): pl.pallas_call(pack_kernel, in_specs=[hbm] * 10, out_shape=[f32(40, 128)]...  1.06 us
  transfers between devices with their start and end apart: 10, of which 5 were waited for; matrix products, arithmetic and copies ran while one was open for 0% of the time, Pallas kernels for 1%

profile of v3, /device:TPU:0, one launch (start us, length us, event | category | flops | bytes accessed | tf_op | source)
XLA Modules:
  0.0 32.3 jit_solution(15826276368603993025)
XLA Ops:
  0.0 1.1 %pack.1 = (f32[40,128]{1,0:T(8,128)S(1)}, f32[40,128]{1,0:T(8,128)S(1)}, f32[56,128]{1,0:T(8,128)S(1)}, f32[56,128]{1,0:T(8,128)S(1)}, f32[344,128]{1,0:T(8,128)...) custom-call(f32[128,128]{1,0:T(8,128)} %bitcast.15, ...), custom_call_target="tpu_custom_call" | custom-call | tf_op jit(solution)/shard_map/pack/pallas_call | solution.py:569
  1.1 0.0 collective-permute-start
  1.1 2.9 %collective-permute-start.1 = (f32[40,128]{1,0:T(8,128)S(1)}, f32[40,128]{1,0:T(8,128)S(1)}, u32[]{:S(2)}, u32[]{:S(2)}) collective-permute-start(f32[40,128]{1,0:T(8,128)S(1)} %get-tuple-element.46), channel_id=1, source_target_pairs={{0,7},{1,0},{2,1},{3,2},{4,3},{5,4},{6,5},{7,6},{8,15},{9,8},{10,9... | collective-permute-start | bytes 61448 | tf_op jit(solution)/shard_map/ppermute | solution.py:540
  4.0 0.0 collective-permute-start.7
  4.0 0.5 %collective-permute-start.8 = (f32[344,128]{1,0:T(8,128)S(1)}, f32[344,128]{1,0:T(8,128)S(1)}, u32[]{:S(2)}, u32[]{:S(2)}) collective-permute-start(f32[344,128]{1,0:T(8,128)S(1)} %get-tuple-element.60), channel_id=1, source_target_pairs={{0,1},{1,0},{2,3},{3,2},{4,5},{5,4},{6,7},{7,6},{8,9},{9,8},{10,11... | collective-permute-start | bytes 528392 | tf_op jit(solution)/shard_map/ppermute | solution.py:540
  4.6 0.9 %collective-permute-done.from_left = f32[40,128]{1,0:T(8,128)S(1)} collective-permute-done((f32[40,128]{1,0:T(8,128)S(1)}, f32[40,128]{1,0:T(8,128)S(1)}, u32[]{:S(2)}, u32[]{:S(2)}) %collective-permute-start) | collective-permute-done | bytes 20512 | tf_op jit(solution)/shard_map/ppermute | solution.py:540
  5.5 0.0 collective-permute-done.1.from_right
  5.5 0.1 slice_select_fusion
  5.6 2.0 %collective-permute-start.2 = (f32[64,128]{1,0:T(8,128)S(1)}, f32[64,128]{1,0:T(8,128)S(1)}, u32[]{:S(2)}, u32[]{:S(2)}) collective-permute-start(f32[64,128]{1,0:T(8,128)S(1)} %get-tuple-element.82), channel_id=1, source_target_pairs={{0,8},{1,9},{2,10},{3,11},{4,12},{5,13},{6,14},{7,15},{8,16},{9,17... | collective-permute-start | bytes 98312 | tf_op jit(solution)/shard_map/ppermute | solution.py:540
  7.6 2.3 %collective-permute-start.3 = (f32[64,128]{1,0:T(8,128)S(1)}, f32[64,128]{1,0:T(8,128)S(1)}, u32[]{:S(2)}, u32[]{:S(2)}) collective-permute-start(f32[64,128]{1,0:T(8,128)S(1)} %get-tuple-element.81), channel_id=1, source_target_pairs={{0,56},{1,57},{2,58},{3,59},{4,60},{5,61},{6,62},{7,63},{8,0},{9,1... | collective-permute-start | bytes 98312 | tf_op jit(solution)/shard_map/ppermute | solution.py:540
  9.9 0.3 collective-permute-start.5
  10.2 1.7 %collective-permute-done.2.from_up = f32[64,128]{1,0:T(8,128)S(1)} collective-permute-done((f32[64,128]{1,0:T(8,128)S(1)}, f32[64,128]{1,0:T(8,128)S(1)}, u32[]{:S(2)}, u32[]{:S(2)}) %collective-permute-start.2) | collective-permute-done | bytes 32800 | tf_op jit(solution)/shard_map/ppermute | solution.py:540
  11.9 0.0 collective-permute-start.6
  11.9 0.3 collective-permute-done.3.from_down
  12.2 0.4 %land.1 = (f32[2,16,256]{2,1,0:T(8,128)S(1)}, f32[8,128]{1,0:T(8,128)S(1)}) custom-call(f32[128,128]{1,0:T(8,128)S(1)} %get-tuple-element.42.water, f32[8,128]{1,0:T(8,128)S(1)} %get-tuple-element.43.soil, f32[16,128]{1,0:T(8,128)S(1)} %get-tuple-element.44.weight, f32[40,128]{1,0:T(8,128)S(1)} %collective-permute-done.from_left, ...), custom_call_target="tpu_custom_call" | custom-call | tf_op jit(solution)/shard_map/land/pallas_call | solution.py:614
  12.6 5.3 %collective-permute-start.4 = (f32[2,16,256]{2,1,0:T(8,128)S(1)}, f32[2,16,256]{2,1,0:T(8,128)S(1)}, u32[]{:S(2)}, u32[]{:S(2)}) collective-permute-start(f32[2,16,256]{2,1,0:T(8,128)S(1)} %get-tuple-element.49), channel_id=1, source_target_pairs={{0,64},{1,65},{2,66},{3,67},{4,68},{5,69},{6,70},{7,71},{8,72},{9,... | collective-permute-start | bytes 98312 | tf_op jit(solution)/shard_map/ppermute | solution.py:540
  17.9 0.0 collective-permute-done.5.from_up
  17.9 0.0 collective-permute-done.6.from_down
  17.9 0.0 collective-permute-done.7.rows_up
  17.9 0.0 collective-permute-done.8.rows_down
  17.9 1.8 %collective-permute-done.4.coarse = f32[2,16,256]{2,1,0:T(8,128)S(1)} collective-permute-done((f32[2,16,256]{2,1,0:T(8,128)S(1)}, f32[2,16,256]{2,1,0:T(8,128)S(1)}, u32[]{:S(2)}, u32[]{:S(2)}) %collective-permute-start.4) | collective-permute-done | bytes 32800 | tf_op jit(solution)/shard_map/ppermute | solution.py:540
  19.8 10.4 %collective-permute-start.9 = (f32[8,128]{1,0:T(8,128)S(1)}, f32[8,128]{1,0:T(8,128)S(1)}, u32[]{:S(2)}, u32[]{:S(2)}) collective-permute-start(f32[8,128]{1,0:T(8,128)S(1)} %get-tuple-element.77), channel_id=1, source_target_pairs={{0,64},{1,65},{2,66},{3,67},{4,68},{5,69},{6,70},{7,71},{8,72},{9,... | collective-permute-start | bytes 12296 | tf_op jit(solution)/shard_map/ppermute | solution.py:540
  30.1 1.6 %collective-permute-done.9 = f32[8,128]{1,0:T(8,128)S(1)} collective-permute-done((f32[8,128]{1,0:T(8,128)S(1)}, f32[8,128]{1,0:T(8,128)S(1)}, u32[]{:S(2)}, u32[]{:S(2)}) %collective-permute-start.9) | collective-permute-done | bytes 4128 | tf_op jit(solution)/shard_map/ppermute | solution.py:540
  31.7 0.6 %fusion.3 = f32[1,8,128]{2,1,0:T(8,128)} fusion(f32[8,128]{1,0:T(8,128)S(1)} %get-tuple-element.78, f32[8,128]{1,0:T(8,128)S(1)} %collective-permute-done.9, f32[8,128]{1,0:T(8,128)S(1)} %get-tuple-element.61.after, pred[]{:T(512)S(6)} %eq.3), kind=kLoop, calls=%fused_computation.8 | loop fusion | flops 5120 | bytes 16385 | tf_op jit(solution)/shard_map/broadcast_in_dim | solution.py:653
  (9 shorter events, 0.1 us)
Async XLA Ops:
  1.1 4.4 %collective-permute-start = (f32[40,128]{1,0:T(8,128)S(1)}, f32[40,128]{1,0:T(8,128)S(1)}, u32[]{:S(2)}, u32[]{:S(2)}) collective-permute-start(f32[40,128]{1,0:T(8,128)S(1)} %get-tuple-element.45), channel_id=1, source_target_pairs={{0,1},{1,2},{2,3},{3,4},{4,5},{5,6},{6,7},{7,0},{8,9},{9,10},{10,1... | collective-permute-start | bytes 61448 | tf_op jit(solution)/shard_map/ppermute | solution.py:540
  1.1 4.4 %collective-permute-start.1 = (f32[40,128]{1,0:T(8,128)S(1)}, f32[40,128]{1,0:T(8,128)S(1)}, u32[]{:S(2)}, u32[]{:S(2)}) collective-permute-start(f32[40,128]{1,0:T(8,128)S(1)} %get-tuple-element.46), channel_id=1, source_target_pairs={{0,7},{1,0},{2,1},{3,2},{4,3},{5,4},{6,5},{7,6},{8,15},{9,8},{10,9... | collective-permute-start | bytes 61448 | tf_op jit(solution)/shard_map/ppermute | solution.py:540
  4.0 13.8 %collective-permute-start.7 = (f32[344,128]{1,0:T(8,128)S(1)}, f32[344,128]{1,0:T(8,128)S(1)}, u32[]{:S(2)}, u32[]{:S(2)}) collective-permute-start(f32[344,128]{1,0:T(8,128)S(1)} %get-tuple-element.59), channel_id=1, source_target_pairs={{0,1},{1,0},{2,3},{3,2},{4,5},{5,4},{6,7},{7,6},{8,9},{9,8},{10,11... | collective-permute-start | bytes 528392 | tf_op jit(solution)/shard_map/ppermute | solution.py:540
  4.0 13.8 %collective-permute-start.8 = (f32[344,128]{1,0:T(8,128)S(1)}, f32[344,128]{1,0:T(8,128)S(1)}, u32[]{:S(2)}, u32[]{:S(2)}) collective-permute-start(f32[344,128]{1,0:T(8,128)S(1)} %get-tuple-element.60), channel_id=1, source_target_pairs={{0,1},{1,0},{2,3},{3,2},{4,5},{5,4},{6,7},{7,6},{8,9},{9,8},{10,11... | collective-permute-start | bytes 528392 | tf_op jit(solution)/shard_map/ppermute | solution.py:540
  5.6 6.3 %collective-permute-start.2 = (f32[64,128]{1,0:T(8,128)S(1)}, f32[64,128]{1,0:T(8,128)S(1)}, u32[]{:S(2)}, u32[]{:S(2)}) collective-permute-start(f32[64,128]{1,0:T(8,128)S(1)} %get-tuple-element.82), channel_id=1, source_target_pairs={{0,8},{1,9},{2,10},{3,11},{4,12},{5,13},{6,14},{7,15},{8,16},{9,17... | collective-permute-start | bytes 98312 | tf_op jit(solution)/shard_map/ppermute | solution.py:540
  7.6 4.6 %collective-permute-start.3 = (f32[64,128]{1,0:T(8,128)S(1)}, f32[64,128]{1,0:T(8,128)S(1)}, u32[]{:S(2)}, u32[]{:S(2)}) collective-permute-start(f32[64,128]{1,0:T(8,128)S(1)} %get-tuple-element.81), channel_id=1, source_target_pairs={{0,56},{1,57},{2,58},{3,59},{4,60},{5,61},{6,62},{7,63},{8,0},{9,1... | collective-permute-start | bytes 98312 | tf_op jit(solution)/shard_map/ppermute | solution.py:540
  9.9 8.0 %collective-permute-start.5 = (f32[72,128]{1,0:T(8,128)S(1)}, f32[72,128]{1,0:T(8,128)S(1)}, u32[]{:S(2)}, u32[]{:S(2)}) collective-permute-start(f32[72,128]{1,0:T(8,128)S(1)} %concatenate.14), channel_id=1, source_target_pairs={{0,1},{1,0},{2,3},{3,2},{4,5},{5,4},{6,7},{7,6},{8,9},{9,8},{10,11... | collective-permute-start | bytes 110600 | tf_op jit(solution)/shard_map/ppermute | solution.py:540
  11.9 6.0 %collective-permute-start.6 = (f32[72,128]{1,0:T(8,128)S(1)}, f32[72,128]{1,0:T(8,128)S(1)}, u32[]{:S(2)}, u32[]{:S(2)}) collective-permute-start(f32[72,128]{1,0:T(8,128)S(1)} %concatenate.15), channel_id=1, source_target_pairs={{0,1},{1,0},{2,3},{3,2},{4,5},{5,4},{6,7},{7,6},{8,9},{9,8},{10,11... | collective-permute-start | bytes 110600 | tf_op jit(solution)/shard_map/ppermute | solution.py:540
  12.6 7.2 %collective-permute-start.4 = (f32[2,16,256]{2,1,0:T(8,128)S(1)}, f32[2,16,256]{2,1,0:T(8,128)S(1)}, u32[]{:S(2)}, u32[]{:S(2)}) collective-permute-start(f32[2,16,256]{2,1,0:T(8,128)S(1)} %get-tuple-element.49), channel_id=1, source_target_pairs={{0,64},{1,65},{2,66},{3,67},{4,68},{5,69},{6,70},{7,71},{8,72},{9,... | collective-permute-start | bytes 98312 | tf_op jit(solution)/shard_map/ppermute | solution.py:540
  19.8 12.0 %collective-permute-start.9 = (f32[8,128]{1,0:T(8,128)S(1)}, f32[8,128]{1,0:T(8,128)S(1)}, u32[]{:S(2)}, u32[]{:S(2)}) collective-permute-start(f32[8,128]{1,0:T(8,128)S(1)} %get-tuple-element.77), channel_id=1, source_target_pairs={{0,64},{1,65},{2,66},{3,67},{4,68},{5,69},{6,70},{7,71},{8,72},{9,... | collective-permute-start | bytes 12296 | tf_op jit(solution)/shard_map/ppermute | solution.py:540

commit v4 on v3

--- a/solution.py
+++ b/solution.py
@@ -73,7 +73,7 @@
 
 def pack_kernel(
     water_in, soil_in, weight_in, etab_in, stab_in, terrain_in, head_in, cond_in, mask_in, code_in,
-    gxl, gxr, main_up, main_down, gyu, gyd, water, soil, weight, tabs, terrain, keff, head, code,
+    gxl, gxr, main_up, main_down, gyu, gyd, extra_up, extra_down, water, soil, weight, tabs, terrain, keff, head, code,
     square, mask, code_int, sems,
 ):
     group = lax.axis_index("comp")
@@ -151,11 +151,10 @@
                 gyu[at : at + 8] = field(slice(0, 8), cut(t))
                 gyd[at : at + 8] = field(slice(ROWS - 8, ROWS), cut(t))
         for t in range(10):
-            at = 320 + 2 * t
-            gyu[at : at + 2] = terrain_at(slice(8, 10), cut(t))
-            gyd[at : at + 2] = terrain_at(slice(ROWS - 10, ROWS - 8), cut(t))
-        gyu[340:344] = jnp.zeros((4, 128), F32)
-        gyd[340:344] = jnp.zeros((4, 128), F32)
+            extra_up[2 * t : 2 * t + 2] = terrain_at(slice(8, 10), cut(t))
+            extra_down[2 * t : 2 * t + 2] = terrain_at(slice(ROWS - 10, ROWS - 8), cut(t))
+        extra_up[20:40] = jnp.zeros((20, 128), F32)
+        extra_down[20:40] = jnp.zeros((20, 128), F32)
         lane = lax.broadcasted_iota(jnp.int32, (ROWS, 128), 1)
         edges = jnp.zeros((ROWS, 128), F32)
         for f, field in enumerate(fields):
@@ -378,10 +377,10 @@
 
         corner = columns_of(3, AGG)
         outer[...] = jnp.zeros((32, WIDE), F32)
-        for at, rows in ((0, rows_down), (16, rows_up)):
+        for at, rows, extra in ((0, rows_down, from_down), (16, rows_up, from_up)):
             for t in range(10):
                 outer[at : at + 8, cut(t)] = rows[240 + t * 8 : 248 + t * 8]
-                outer[at + 8 : at + 10, cut(t)] = rows[320 + t * 2 : 322 + t * 2]
+                outer[at + 8 : at + 10, cut(t)] = extra[40 + t * 2 : 42 + t * 2]
         outer[0:10, cut(10)] = corner[80:90]
         outer[16:24, cut(10)] = corner[96:104]
         outer[24:26, cut(10)] = corner[94:96]
@@ -566,12 +565,13 @@
     hbm = pl.BlockSpec(memory_space=pltpu.HBM)
     fine = f32(ROWS, COLS)
     fine_int = pltpu.VMEM((ROWS, COLS), jnp.int32)
-    gxl, gxr, main_up, main_down, gyu, gyd, water, soil, weight, tabs, terrain, keff, head, code = pl.pallas_call(
+    gxl, gxr, main_up, main_down, gyu, gyd, extra_up, extra_down, water, soil, weight, tabs, terrain, keff, head, code = pl.pallas_call(
         pack_kernel,
         in_specs=[hbm] * 10,
         out_shape=[f32(40, 128)] * 2
         + [f32(56, 128)] * 2
-        + [f32(344, 128)] * 2
+        + [f32(320, 128)] * 2
+        + [f32(40, 128)] * 2
         + [f32(128, 128), f32(8, 128), f32(LEV, 128), f32(3, 1, NW)]
         + [jax.ShapeDtypeStruct((ROWS, COLS), jnp.int32)]
         + [fine] * 3,
@@ -606,10 +606,10 @@
     )
     lane = lax.broadcasted_iota(jnp.int32, (40, 128), 1)
     route_up = moved(
-        jnp.concatenate([jnp.where(lane < 100, from_right, from_left), jnp.zeros((32, 128), F32)]), shape, lambda g, y, x: (g, y + 1, x) if g else (g, y, x ^ 1)
+        jnp.concatenate([jnp.where(lane < 100, from_right, from_left), extra_down]), shape, lambda g, y, x: (g, y + 1, x) if g else (g, y, x ^ 1)
     )
     route_down = moved(
-        jnp.concatenate([jnp.where(lane < 40, from_right, from_left), jnp.zeros((32, 128), F32)]), shape, lambda g, y, x: (g, y - 1, x) if g else (g, y, x ^ 1)
+        jnp.concatenate([jnp.where(lane < 40, from_right, from_left), extra_up]), shape, lambda g, y, x: (g, y - 1, x) if g else (g, y, x ^ 1)
     )
     coarse, water_top = pl.pallas_call(
         land_kernel,

time: 32.5 us -> 32.5 us (level)
  no operation moved by 1% of the time
where the time goes in v4:
time: 32.5 us; the launch traced here: 32.3 us
  starting transfers between devices  23.7 us (73%)
  waiting for transfers between devices  6.39 us (20%)
  Pallas kernels  1.52 us (5%)
  other arithmetic  0.71 us (2%)
    ppermute x10, starting transfers between devices, moved(): return lax.ppermute(array, ('comp', 'gy', 'gx'), pairs)  23.7 us
    ppermute x10, waiting for transfers between devices, moved(): return lax.ppermute(array, ('comp', 'gy', 'gx'), pairs)  6.39 us
    pallas_call x1, Pallas kernels, per_device(): pl.pallas_call(pack_kernel, in_specs=[hbm] * 10, out_shape=[f32(40, 128)]...  1.06 us
  transfers between devices with their start and end apart: 10, of which 5 were waited for; matrix products, arithmetic and copies ran while one was open for 0% of the time, Pallas kernels for 1%

profile of v4, /device:TPU:0, one launch (start us, length us, event | category | flops | bytes accessed | tf_op | source)
XLA Modules:
  0.0 32.3 jit_solution(6795521483460888328)
XLA Ops:
  0.0 1.1 %pack.1 = (f32[40,128]{1,0:T(8,128)S(1)}, f32[40,128]{1,0:T(8,128)S(1)}, f32[56,128]{1,0:T(8,128)S(1)}, f32[56,128]{1,0:T(8,128)S(1)}, f32[320,128]{1,0:T(8,128)...) custom-call(f32[128,128]{1,0:T(8,128)} %bitcast.15, ...), custom_call_target="tpu_custom_call" | custom-call | tf_op jit(solution)/shard_map/pack/pallas_call | solution.py:568
  1.1 0.0 collective-permute-start
  1.1 2.9 %collective-permute-start.1 = (f32[40,128]{1,0:T(8,128)S(1)}, f32[40,128]{1,0:T(8,128)S(1)}, u32[]{:S(2)}, u32[]{:S(2)}) collective-permute-start(f32[40,128]{1,0:T(8,128)S(1)} %get-tuple-element.48), channel_id=1, source_target_pairs={{0,7},{1,0},{2,1},{3,2},{4,3},{5,4},{6,5},{7,6},{8,15},{9,8},{10,9... | collective-permute-start | bytes 61448 | tf_op jit(solution)/shard_map/ppermute | solution.py:539
  4.0 0.0 collective-permute-start.7
  4.0 0.5 %collective-permute-start.8 = (f32[320,128]{1,0:T(8,128)S(1)}, f32[320,128]{1,0:T(8,128)S(1)}, u32[]{:S(2)}, u32[]{:S(2)}) collective-permute-start(f32[320,128]{1,0:T(8,128)S(1)} %get-tuple-element.64), channel_id=1, source_target_pairs={{0,1},{1,0},{2,3},{3,2},{4,5},{5,4},{6,7},{7,6},{8,9},{9,8},{10,11... | collective-permute-start | bytes 491528 | tf_op jit(solution)/shard_map/ppermute | solution.py:539
  4.6 0.9 %collective-permute-done.from_left = f32[40,128]{1,0:T(8,128)S(1)} collective-permute-done((f32[40,128]{1,0:T(8,128)S(1)}, f32[40,128]{1,0:T(8,128)S(1)}, u32[]{:S(2)}, u32[]{:S(2)}) %collective-permute-start) | collective-permute-done | bytes 20512 | tf_op jit(solution)/shard_map/ppermute | solution.py:539
  5.5 0.0 collective-permute-done.1.from_right
  5.5 0.1 slice_select_fusion
  5.6 2.0 %collective-permute-start.2 = (f32[64,128]{1,0:T(8,128)S(1)}, f32[64,128]{1,0:T(8,128)S(1)}, u32[]{:S(2)}, u32[]{:S(2)}) collective-permute-start(f32[64,128]{1,0:T(8,128)S(1)} %get-tuple-element.86), channel_id=1, source_target_pairs={{0,8},{1,9},{2,10},{3,11},{4,12},{5,13},{6,14},{7,15},{8,16},{9,17... | collective-permute-start | bytes 98312 | tf_op jit(solution)/shard_map/ppermute | solution.py:539
  7.6 2.3 %collective-permute-start.3 = (f32[64,128]{1,0:T(8,128)S(1)}, f32[64,128]{1,0:T(8,128)S(1)}, u32[]{:S(2)}, u32[]{:S(2)}) collective-permute-start(f32[64,128]{1,0:T(8,128)S(1)} %get-tuple-element.85), channel_id=1, source_target_pairs={{0,56},{1,57},{2,58},{3,59},{4,60},{5,61},{6,62},{7,63},{8,0},{9,1... | collective-permute-start | bytes 98312 | tf_op jit(solution)/shard_map/ppermute | solution.py:539
  9.9 0.3 collective-permute-start.5
  10.2 1.7 %collective-permute-done.2.from_up = f32[64,128]{1,0:T(8,128)S(1)} collective-permute-done((f32[64,128]{1,0:T(8,128)S(1)}, f32[64,128]{1,0:T(8,128)S(1)}, u32[]{:S(2)}, u32[]{:S(2)}) %collective-permute-start.2) | collective-permute-done | bytes 32800 | tf_op jit(solution)/shard_map/ppermute | solution.py:539
  11.9 0.0 collective-permute-start.6
  11.9 0.3 collective-permute-done.3.from_down
  12.2 0.4 %land.1 = (f32[2,16,256]{2,1,0:T(8,128)S(1)}, f32[8,128]{1,0:T(8,128)S(1)}) custom-call(f32[128,128]{1,0:T(8,128)S(1)} %get-tuple-element.44.water, f32[8,128]{1,0:T(8,128)S(1)} %get-tuple-element.45.soil, f32[16,128]{1,0:T(8,128)S(1)} %get-tuple-element.46.weight, f32[40,128]{1,0:T(8,128)S(1)} %collective-permute-done.from_left, ...), custom_call_target="tpu_custom_call" | custom-call | tf_op jit(solution)/shard_map/land/pallas_call | solution.py:614
  12.6 5.3 %collective-permute-start.4 = (f32[2,16,256]{2,1,0:T(8,128)S(1)}, f32[2,16,256]{2,1,0:T(8,128)S(1)}, u32[]{:S(2)}, u32[]{:S(2)}) collective-permute-start(f32[2,16,256]{2,1,0:T(8,128)S(1)} %get-tuple-element.51), channel_id=1, source_target_pairs={{0,64},{1,65},{2,66},{3,67},{4,68},{5,69},{6,70},{7,71},{8,72},{9,... | collective-permute-start | bytes 98312 | tf_op jit(solution)/shard_map/ppermute | solution.py:539
  17.9 0.0 collective-permute-done.5.from_up
  17.9 0.0 collective-permute-done.6.from_down
  17.9 0.0 collective-permute-done.7.rows_up
  17.9 0.0 collective-permute-done.8.rows_down
  17.9 1.8 %collective-permute-done.4.coarse = f32[2,16,256]{2,1,0:T(8,128)S(1)} collective-permute-done((f32[2,16,256]{2,1,0:T(8,128)S(1)}, f32[2,16,256]{2,1,0:T(8,128)S(1)}, u32[]{:S(2)}, u32[]{:S(2)}) %collective-permute-start.4) | collective-permute-done | bytes 32800 | tf_op jit(solution)/shard_map/ppermute | solution.py:539
  19.8 10.4 %collective-permute-start.9 = (f32[8,128]{1,0:T(8,128)S(1)}, f32[8,128]{1,0:T(8,128)S(1)}, u32[]{:S(2)}, u32[]{:S(2)}) collective-permute-start(f32[8,128]{1,0:T(8,128)S(1)} %get-tuple-element.81), channel_id=1, source_target_pairs={{0,64},{1,65},{2,66},{3,67},{4,68},{5,69},{6,70},{7,71},{8,72},{9,... | collective-permute-start | bytes 12296 | tf_op jit(solution)/shard_map/ppermute | solution.py:539
  30.1 1.6 %collective-permute-done.9 = f32[8,128]{1,0:T(8,128)S(1)} collective-permute-done((f32[8,128]{1,0:T(8,128)S(1)}, f32[8,128]{1,0:T(8,128)S(1)}, u32[]{:S(2)}, u32[]{:S(2)}) %collective-permute-start.9) | collective-permute-done | bytes 4128 | tf_op jit(solution)/shard_map/ppermute | solution.py:539
  31.7 0.6 %fusion.3 = f32[1,8,128]{2,1,0:T(8,128)} fusion(f32[8,128]{1,0:T(8,128)S(1)} %get-tuple-element.82, f32[8,128]{1,0:T(8,128)S(1)} %collective-permute-done.9, f32[8,128]{1,0:T(8,128)S(1)} %get-tuple-element.65.after, pred[]{:T(512)S(6)} %eq.3), kind=kLoop, calls=%fused_computation.10 | loop fusion | flops 5120 | bytes 16385 | tf_op jit(solution)/shard_map/broadcast_in_dim | solution.py:653
  (9 shorter events, 0.1 us)
Async XLA Ops:
  1.1 4.4 %collective-permute-start = (f32[40,128]{1,0:T(8,128)S(1)}, f32[40,128]{1,0:T(8,128)S(1)}, u32[]{:S(2)}, u32[]{:S(2)}) collective-permute-start(f32[40,128]{1,0:T(8,128)S(1)} %get-tuple-element.47), channel_id=1, source_target_pairs={{0,1},{1,2},{2,3},{3,4},{4,5},{5,6},{6,7},{7,0},{8,9},{9,10},{10,1... | collective-permute-start | bytes 61448 | tf_op jit(solution)/shard_map/ppermute | solution.py:539
  1.1 4.4 %collective-permute-start.1 = (f32[40,128]{1,0:T(8,128)S(1)}, f32[40,128]{1,0:T(8,128)S(1)}, u32[]{:S(2)}, u32[]{:S(2)}) collective-permute-start(f32[40,128]{1,0:T(8,128)S(1)} %get-tuple-element.48), channel_id=1, source_target_pairs={{0,7},{1,0},{2,1},{3,2},{4,3},{5,4},{6,5},{7,6},{8,15},{9,8},{10,9... | collective-permute-start | bytes 61448 | tf_op jit(solution)/shard_map/ppermute | solution.py:539
  4.0 13.8 %collective-permute-start.7 = (f32[320,128]{1,0:T(8,128)S(1)}, f32[320,128]{1,0:T(8,128)S(1)}, u32[]{:S(2)}, u32[]{:S(2)}) collective-permute-start(f32[320,128]{1,0:T(8,128)S(1)} %get-tuple-element.63), channel_id=1, source_target_pairs={{0,1},{1,0},{2,3},{3,2},{4,5},{5,4},{6,7},{7,6},{8,9},{9,8},{10,11... | collective-permute-start | bytes 491528 | tf_op jit(solution)/shard_map/ppermute | solution.py:539
  4.0 13.8 %collective-permute-start.8 = (f32[320,128]{1,0:T(8,128)S(1)}, f32[320,128]{1,0:T(8,128)S(1)}, u32[]{:S(2)}, u32[]{:S(2)}) collective-permute-start(f32[320,128]{1,0:T(8,128)S(1)} %get-tuple-element.64), channel_id=1, source_target_pairs={{0,1},{1,0},{2,3},{3,2},{4,5},{5,4},{6,7},{7,6},{8,9},{9,8},{10,11... | collective-permute-start | bytes 491528 | tf_op jit(solution)/shard_map/ppermute | solution.py:539
  5.6 6.3 %collective-permute-start.2 = (f32[64,128]{1,0:T(8,128)S(1)}, f32[64,128]{1,0:T(8,128)S(1)}, u32[]{:S(2)}, u32[]{:S(2)}) collective-permute-start(f32[64,128]{1,0:T(8,128)S(1)} %get-tuple-element.86), channel_id=1, source_target_pairs={{0,8},{1,9},{2,10},{3,11},{4,12},{5,13},{6,14},{7,15},{8,16},{9,17... | collective-permute-start | bytes 98312 | tf_op jit(solution)/shard_map/ppermute | solution.py:539
  7.6 4.6 %collective-permute-start.3 = (f32[64,128]{1,0:T(8,128)S(1)}, f32[64,128]{1,0:T(8,128)S(1)}, u32[]{:S(2)}, u32[]{:S(2)}) collective-permute-start(f32[64,128]{1,0:T(8,128)S(1)} %get-tuple-element.85), channel_id=1, source_target_pairs={{0,56},{1,57},{2,58},{3,59},{4,60},{5,61},{6,62},{7,63},{8,0},{9,1... | collective-permute-start | bytes 98312 | tf_op jit(solution)/shard_map/ppermute | solution.py:539
  9.9 8.0 %collective-permute-start.5 = (f32[80,128]{1,0:T(8,128)S(1)}, f32[80,128]{1,0:T(8,128)S(1)}, u32[]{:S(2)}, u32[]{:S(2)}) collective-permute-start(f32[80,128]{1,0:T(8,128)S(1)} %pad_maximum_fusion.2), channel_id=1, source_target_pairs={{0,1},{1,0},{2,3},{3,2},{4,5},{5,4},{6,7},{7,6},{8,9},{9,8},{10,11... | collective-permute-start | bytes 122888 | tf_op jit(solution)/shard_map/ppermute | solution.py:539
  11.9 6.0 %collective-permute-start.6 = (f32[80,128]{1,0:T(8,128)S(1)}, f32[80,128]{1,0:T(8,128)S(1)}, u32[]{:S(2)}, u32[]{:S(2)}) collective-permute-start(f32[80,128]{1,0:T(8,128)S(1)} %pad_maximum_fusion.3), channel_id=1, source_target_pairs={{0,1},{1,0},{2,3},{3,2},{4,5},{5,4},{6,7},{7,6},{8,9},{9,8},{10,11... | collective-permute-start | bytes 122888 | tf_op jit(solution)/shard_map/ppermute | solution.py:539
  12.6 7.2 %collective-permute-start.4 = (f32[2,16,256]{2,1,0:T(8,128)S(1)}, f32[2,16,256]{2,1,0:T(8,128)S(1)}, u32[]{:S(2)}, u32[]{:S(2)}) collective-permute-start(f32[2,16,256]{2,1,0:T(8,128)S(1)} %get-tuple-element.51), channel_id=1, source_target_pairs={{0,64},{1,65},{2,66},{3,67},{4,68},{5,69},{6,70},{7,71},{8,72},{9,... | collective-permute-start | bytes 98312 | tf_op jit(solution)/shard_map/ppermute | solution.py:539
  19.8 12.0 %collective-permute-start.9 = (f32[8,128]{1,0:T(8,128)S(1)}, f32[8,128]{1,0:T(8,128)S(1)}, u32[]{:S(2)}, u32[]{:S(2)}) collective-permute-start(f32[8,128]{1,0:T(8,128)S(1)} %get-tuple-element.81), channel_id=1, source_target_pairs={{0,64},{1,65},{2,66},{3,67},{4,68},{5,69},{6,70},{7,71},{8,72},{9,... | collective-permute-start | bytes 12296 | tf_op jit(solution)/shard_map/ppermute | solution.py:539

commit v5 on v4

--- a/solution.py
+++ b/solution.py
@@ -117,7 +117,7 @@
         ]
         loads = []
         for i, (source, target) in enumerate(
-            ((terrain_in, terrain), (cond_in, keff), (mask_in, mask), (head_in, head), (code_in, code_int))
+            ((cond_in, keff), (mask_in, mask), (code_in, code_int), (head_in, head), (terrain_in, terrain))
         ):
             parts = []
             for j in range(CHUNKS):
@@ -133,13 +133,13 @@
             for part in loads[i]:
                 part.wait()
 
+        ready(0)
         ready(1)
+        keff[...] = keff[...] * mask[...].astype(F32)
         ready(2)
-        keff[...] = keff[...] * mask[...].astype(F32)
-        ready(4)
         code[...] = code_int[...].astype(F32)
         ready(3)
-        ready(0)
+        ready(4)
 
         def terrain_at(r, c):
             return terrain[r, c].astype(F32)

time: 32.5 us -> 32.4 us (level)
  no operation moved by 1% of the time
where the time goes in v5:
time: 32.4 us; the launch traced here: 32.3 us
  starting transfers between devices  23.6 us (73%)
  waiting for transfers between devices  6.39 us (20%)
  Pallas kernels  1.52 us (5%)
  other arithmetic  0.71 us (2%)
    ppermute x10, starting transfers between devices, moved(): return lax.ppermute(array, ('comp', 'gy', 'gx'), pairs)  23.6 us
    ppermute x10, waiting for transfers between devices, moved(): return lax.ppermute(array, ('comp', 'gy', 'gx'), pairs)  6.39 us
    pallas_call x1, Pallas kernels, per_device(): pl.pallas_call(pack_kernel, in_specs=[hbm] * 10, out_shape=[f32(40, 128)]...  1.06 us
  transfers between devices with their start and end apart: 10, of which 5 were waited for; matrix products, arithmetic and copies ran while one was open for 0% of the time, Pallas kernels for 1%

profile of v5, /device:TPU:0, one launch (start us, length us, event | category | flops | bytes accessed | tf_op | source)
XLA Modules:
  0.0 32.3 jit_solution(635293575681365566)
XLA Ops:
  0.0 1.1 %pack.1 = (f32[40,128]{1,0:T(8,128)S(1)}, f32[40,128]{1,0:T(8,128)S(1)}, f32[56,128]{1,0:T(8,128)S(1)}, f32[56,128]{1,0:T(8,128)S(1)}, f32[320,128]{1,0:T(8,128)...) custom-call(f32[128,128]{1,0:T(8,128)} %bitcast.15, ...), custom_call_target="tpu_custom_call" | custom-call | tf_op jit(solution)/shard_map/pack/pallas_call | solution.py:568
  1.1 0.0 collective-permute-start
  1.1 2.9 %collective-permute-start.1 = (f32[40,128]{1,0:T(8,128)S(1)}, f32[40,128]{1,0:T(8,128)S(1)}, u32[]{:S(2)}, u32[]{:S(2)}) collective-permute-start(f32[40,128]{1,0:T(8,128)S(1)} %get-tuple-element.48), channel_id=1, source_target_pairs={{0,7},{1,0},{2,1},{3,2},{4,3},{5,4},{6,5},{7,6},{8,15},{9,8},{10,9... | collective-permute-start | bytes 61448 | tf_op jit(solution)/shard_map/ppermute | solution.py:539
  4.0 0.0 collective-permute-start.7
  4.0 0.5 %collective-permute-start.8 = (f32[320,128]{1,0:T(8,128)S(1)}, f32[320,128]{1,0:T(8,128)S(1)}, u32[]{:S(2)}, u32[]{:S(2)}) collective-permute-start(f32[320,128]{1,0:T(8,128)S(1)} %get-tuple-element.64), channel_id=1, source_target_pairs={{0,1},{1,0},{2,3},{3,2},{4,5},{5,4},{6,7},{7,6},{8,9},{9,8},{10,11... | collective-permute-start | bytes 491528 | tf_op jit(solution)/shard_map/ppermute | solution.py:539
  4.6 0.9 %collective-permute-done.from_left = f32[40,128]{1,0:T(8,128)S(1)} collective-permute-done((f32[40,128]{1,0:T(8,128)S(1)}, f32[40,128]{1,0:T(8,128)S(1)}, u32[]{:S(2)}, u32[]{:S(2)}) %collective-permute-start) | collective-permute-done | bytes 20512 | tf_op jit(solution)/shard_map/ppermute | solution.py:539
  5.5 0.0 collective-permute-done.1.from_right
  5.5 0.1 slice_select_fusion
  5.6 2.0 %collective-permute-start.2 = (f32[64,128]{1,0:T(8,128)S(1)}, f32[64,128]{1,0:T(8,128)S(1)}, u32[]{:S(2)}, u32[]{:S(2)}) collective-permute-start(f32[64,128]{1,0:T(8,128)S(1)} %get-tuple-element.86), channel_id=1, source_target_pairs={{0,8},{1,9},{2,10},{3,11},{4,12},{5,13},{6,14},{7,15},{8,16},{9,17... | collective-permute-start | bytes 98312 | tf_op jit(solution)/shard_map/ppermute | solution.py:539
  7.6 2.3 %collective-permute-start.3 = (f32[64,128]{1,0:T(8,128)S(1)}, f32[64,128]{1,0:T(8,128)S(1)}, u32[]{:S(2)}, u32[]{:S(2)}) collective-permute-start(f32[64,128]{1,0:T(8,128)S(1)} %get-tuple-element.85), channel_id=1, source_target_pairs={{0,56},{1,57},{2,58},{3,59},{4,60},{5,61},{6,62},{7,63},{8,0},{9,1... | collective-permute-start | bytes 98312 | tf_op jit(solution)/shard_map/ppermute | solution.py:539
  9.9 0.3 collective-permute-start.5
  10.2 1.7 %collective-permute-done.2.from_up = f32[64,128]{1,0:T(8,128)S(1)} collective-permute-done((f32[64,128]{1,0:T(8,128)S(1)}, f32[64,128]{1,0:T(8,128)S(1)}, u32[]{:S(2)}, u32[]{:S(2)}) %collective-permute-start.2) | collective-permute-done | bytes 32800 | tf_op jit(solution)/shard_map/ppermute | solution.py:539
  11.9 0.0 collective-permute-start.6
  11.9 0.3 collective-permute-done.3.from_down
  12.2 0.4 %land.1 = (f32[2,16,256]{2,1,0:T(8,128)S(1)}, f32[8,128]{1,0:T(8,128)S(1)}) custom-call(f32[128,128]{1,0:T(8,128)S(1)} %get-tuple-element.44.water, f32[8,128]{1,0:T(8,128)S(1)} %get-tuple-element.45.soil, f32[16,128]{1,0:T(8,128)S(1)} %get-tuple-element.46.weight, f32[40,128]{1,0:T(8,128)S(1)} %collective-permute-done.from_left, ...), custom_call_target="tpu_custom_call" | custom-call | tf_op jit(solution)/shard_map/land/pallas_call | solution.py:614
  12.6 5.2 %collective-permute-start.4 = (f32[2,16,256]{2,1,0:T(8,128)S(1)}, f32[2,16,256]{2,1,0:T(8,128)S(1)}, u32[]{:S(2)}, u32[]{:S(2)}) collective-permute-start(f32[2,16,256]{2,1,0:T(8,128)S(1)} %get-tuple-element.51), channel_id=1, source_target_pairs={{0,64},{1,65},{2,66},{3,67},{4,68},{5,69},{6,70},{7,71},{8,72},{9,... | collective-permute-start | bytes 98312 | tf_op jit(solution)/shard_map/ppermute | solution.py:539
  17.8 0.0 collective-permute-done.5.from_up
  17.8 0.0 collective-permute-done.6.from_down
  17.8 0.0 collective-permute-done.7.rows_up
  17.9 0.0 collective-permute-done.8.rows_down
  17.9 1.8 %collective-permute-done.4.coarse = f32[2,16,256]{2,1,0:T(8,128)S(1)} collective-permute-done((f32[2,16,256]{2,1,0:T(8,128)S(1)}, f32[2,16,256]{2,1,0:T(8,128)S(1)}, u32[]{:S(2)}, u32[]{:S(2)}) %collective-permute-start.4) | collective-permute-done | bytes 32800 | tf_op jit(solution)/shard_map/ppermute | solution.py:539
  19.7 10.4 %collective-permute-start.9 = (f32[8,128]{1,0:T(8,128)S(1)}, f32[8,128]{1,0:T(8,128)S(1)}, u32[]{:S(2)}, u32[]{:S(2)}) collective-permute-start(f32[8,128]{1,0:T(8,128)S(1)} %get-tuple-element.81), channel_id=1, source_target_pairs={{0,64},{1,65},{2,66},{3,67},{4,68},{5,69},{6,70},{7,71},{8,72},{9,... | collective-permute-start | bytes 12296 | tf_op jit(solution)/shard_map/ppermute | solution.py:539
  30.1 1.6 %collective-permute-done.9 = f32[8,128]{1,0:T(8,128)S(1)} collective-permute-done((f32[8,128]{1,0:T(8,128)S(1)}, f32[8,128]{1,0:T(8,128)S(1)}, u32[]{:S(2)}, u32[]{:S(2)}) %collective-permute-start.9) | collective-permute-done | bytes 4128 | tf_op jit(solution)/shard_map/ppermute | solution.py:539
  31.7 0.6 %fusion.3 = f32[1,8,128]{2,1,0:T(8,128)} fusion(f32[8,128]{1,0:T(8,128)S(1)} %get-tuple-element.82, f32[8,128]{1,0:T(8,128)S(1)} %collective-permute-done.9, f32[8,128]{1,0:T(8,128)S(1)} %get-tuple-element.65.after, pred[]{:T(512)S(6)} %eq.3), kind=kLoop, calls=%fused_computation.10 | loop fusion | flops 5120 | bytes 16385 | tf_op jit(solution)/shard_map/broadcast_in_dim | solution.py:653
  (9 shorter events, 0.1 us)
Async XLA Ops:
  1.1 4.4 %collective-permute-start = (f32[40,128]{1,0:T(8,128)S(1)}, f32[40,128]{1,0:T(8,128)S(1)}, u32[]{:S(2)}, u32[]{:S(2)}) collective-permute-start(f32[40,128]{1,0:T(8,128)S(1)} %get-tuple-element.47), channel_id=1, source_target_pairs={{0,1},{1,2},{2,3},{3,4},{4,5},{5,6},{6,7},{7,0},{8,9},{9,10},{10,1... | collective-permute-start | bytes 61448 | tf_op jit(solution)/shard_map/ppermute | solution.py:539
  1.1 4.4 %collective-permute-start.1 = (f32[40,128]{1,0:T(8,128)S(1)}, f32[40,128]{1,0:T(8,128)S(1)}, u32[]{:S(2)}, u32[]{:S(2)}) collective-permute-start(f32[40,128]{1,0:T(8,128)S(1)} %get-tuple-element.48), channel_id=1, source_target_pairs={{0,7},{1,0},{2,1},{3,2},{4,3},{5,4},{6,5},{7,6},{8,15},{9,8},{10,9... | collective-permute-start | bytes 61448 | tf_op jit(solution)/shard_map/ppermute | solution.py:539
  4.0 13.8 %collective-permute-start.7 = (f32[320,128]{1,0:T(8,128)S(1)}, f32[320,128]{1,0:T(8,128)S(1)}, u32[]{:S(2)}, u32[]{:S(2)}) collective-permute-start(f32[320,128]{1,0:T(8,128)S(1)} %get-tuple-element.63), channel_id=1, source_target_pairs={{0,1},{1,0},{2,3},{3,2},{4,5},{5,4},{6,7},{7,6},{8,9},{9,8},{10,11... | collective-permute-start | bytes 491528 | tf_op jit(solution)/shard_map/ppermute | solution.py:539
  4.0 13.8 %collective-permute-start.8 = (f32[320,128]{1,0:T(8,128)S(1)}, f32[320,128]{1,0:T(8,128)S(1)}, u32[]{:S(2)}, u32[]{:S(2)}) collective-permute-start(f32[320,128]{1,0:T(8,128)S(1)} %get-tuple-element.64), channel_id=1, source_target_pairs={{0,1},{1,0},{2,3},{3,2},{4,5},{5,4},{6,7},{7,6},{8,9},{9,8},{10,11... | collective-permute-start | bytes 491528 | tf_op jit(solution)/shard_map/ppermute | solution.py:539
  5.6 6.3 %collective-permute-start.2 = (f32[64,128]{1,0:T(8,128)S(1)}, f32[64,128]{1,0:T(8,128)S(1)}, u32[]{:S(2)}, u32[]{:S(2)}) collective-permute-start(f32[64,128]{1,0:T(8,128)S(1)} %get-tuple-element.86), channel_id=1, source_target_pairs={{0,8},{1,9},{2,10},{3,11},{4,12},{5,13},{6,14},{7,15},{8,16},{9,17... | collective-permute-start | bytes 98312 | tf_op jit(solution)/shard_map/ppermute | solution.py:539
  7.6 4.6 %collective-permute-start.3 = (f32[64,128]{1,0:T(8,128)S(1)}, f32[64,128]{1,0:T(8,128)S(1)}, u32[]{:S(2)}, u32[]{:S(2)}) collective-permute-start(f32[64,128]{1,0:T(8,128)S(1)} %get-tuple-element.85), channel_id=1, source_target_pairs={{0,56},{1,57},{2,58},{3,59},{4,60},{5,61},{6,62},{7,63},{8,0},{9,1... | collective-permute-start | bytes 98312 | tf_op jit(solution)/shard_map/ppermute | solution.py:539
  9.9 7.9 %collective-permute-start.5 = (f32[80,128]{1,0:T(8,128)S(1)}, f32[80,128]{1,0:T(8,128)S(1)}, u32[]{:S(2)}, u32[]{:S(2)}) collective-permute-start(f32[80,128]{1,0:T(8,128)S(1)} %pad_maximum_fusion.2), channel_id=1, source_target_pairs={{0,1},{1,0},{2,3},{3,2},{4,5},{5,4},{6,7},{7,6},{8,9},{9,8},{10,11... | collective-permute-start | bytes 122888 | tf_op jit(solution)/shard_map/ppermute | solution.py:539
  11.9 6.0 %collective-permute-start.6 = (f32[80,128]{1,0:T(8,128)S(1)}, f32[80,128]{1,0:T(8,128)S(1)}, u32[]{:S(2)}, u32[]{:S(2)}) collective-permute-start(f32[80,128]{1,0:T(8,128)S(1)} %pad_maximum_fusion.3), channel_id=1, source_target_pairs={{0,1},{1,0},{2,3},{3,2},{4,5},{5,4},{6,7},{7,6},{8,9},{9,8},{10,11... | collective-permute-start | bytes 122888 | tf_op jit(solution)/shard_map/ppermute | solution.py:539
  12.6 7.1 %collective-permute-start.4 = (f32[2,16,256]{2,1,0:T(8,128)S(1)}, f32[2,16,256]{2,1,0:T(8,128)S(1)}, u32[]{:S(2)}, u32[]{:S(2)}) collective-permute-start(f32[2,16,256]{2,1,0:T(8,128)S(1)} %get-tuple-element.51), channel_id=1, source_target_pairs={{0,64},{1,65},{2,66},{3,67},{4,68},{5,69},{6,70},{7,71},{8,72},{9,... | collective-permute-start | bytes 98312 | tf_op jit(solution)/shard_map/ppermute | solution.py:539
  19.7 12.0 %collective-permute-start.9 = (f32[8,128]{1,0:T(8,128)S(1)}, f32[8,128]{1,0:T(8,128)S(1)}, u32[]{:S(2)}, u32[]{:S(2)}) collective-permute-start(f32[8,128]{1,0:T(8,128)S(1)} %get-tuple-element.81), channel_id=1, source_target_pairs={{0,64},{1,65},{2,66},{3,67},{4,68},{5,69},{6,70},{7,71},{8,72},{9,... | collective-permute-start | bytes 12296 | tf_op jit(solution)/shard_map/ppermute | solution.py:539
